TPU v7x, 32 devices: a whole 2x2x4 slice. The times are simulated.
32 devices in a mesh: dp: 4 (over z), fsdp: 8 (over y, x, core).
Axes of the slice: x: 2, y: 2, z: 4, core: 2. Of those that a mesh axis runs over, the one named last changes fastest.
Arguments:
- tokens: bfloat16 [32768, 1024], P(('dp', 'fsdp')), may hold values from -6 to 6
- norm_gain: bfloat16 [2, 1024], P(None, ('dp', 'fsdp')), may hold values from 0.5 to 1.5
- norm_bias: bfloat16 [2, 1024], P(None, ('dp', 'fsdp')), may hold values from -1 to 1
- w_qkv: bfloat16 [1024, 3072], P(('dp', 'fsdp')), may hold values from -0.1875 to 0.1875
- attn_bias: bfloat16 [3, 1024], P(None, ('dp', 'fsdp')), may hold values from -1 to 1
- w_attn_out: bfloat16 [1024, 1024], P(('dp', 'fsdp')), may hold values from -0.75 to 0.75
- expert_in: bfloat16 [2, 1024, 4096], P(None, ('dp', 'fsdp')), may hold values from -0.1875 to 0.1875
- expert_in_bias: bfloat16 [2, 4096], P(None, ('dp', 'fsdp')), may hold values from -1 to 1
- expert_out: bfloat16 [2, 4096, 1024], P(None, ('dp', 'fsdp')), may hold values from -0.125 to 0.125
- expert_out_bias: bfloat16 [2, 1024], P(None, ('dp', 'fsdp')), may hold values from -1 to 1
- expert_ids: int32 [32768, 1], P(('dp', 'fsdp')), may hold values from 0 to 1, as said below
- running_load: float32 [2], replicated, may hold values from 0.5 to 1.5
- cotangent: bfloat16 [32768, 1024], P(('dp', 'fsdp')), may hold values from -6 to 6
Outputs:
- block_out: bfloat16 [32768, 1024], P(('dp', 'fsdp'))
- input_grad: float32 [32768, 1024], P(('dp', 'fsdp'))
- norm_gain_grad: float32 [2, 1024], P(None, ('dp', 'fsdp'))
- norm_bias_grad: float32 [2, 1024], P(None, ('dp', 'fsdp'))
- qkv_grad: float32 [1024, 3072], P(('dp', 'fsdp'))
- attn_bias_grad: float32 [3, 1024], P(None, ('dp', 'fsdp'))
- attn_out_grad: float32 [1024, 1024], P(('dp', 'fsdp'))
- expert_in_grad: float32 [2, 1024, 4096], P(None, ('dp', 'fsdp'))
- expert_in_bias_grad: float32 [2, 4096], P(None, ('dp', 'fsdp'))
- expert_out_grad: float32 [2, 4096, 1024], P(None, ('dp', 'fsdp'))
- expert_out_bias_grad: float32 [2, 1024], P(None, ('dp', 'fsdp'))
- expert_counts: int32 [2], replicated
- expert_load: float32 [2], replicated
Inputs may be any that keep to these rules, and one draw needn't show every extreme that they name: `expert_ids`: among the tokens of one device no expert is named more than 640 times; in some device's tokens some expert is named exactly 640 times.
All inputs are finite; a program needn't handle non-finite values.
Results may differ from a plain program's by a relative error of at most 0.0095.
Values may be sent and summed in bfloat16 or wider, within the bound.
A program may use at most 448 MiB of HBM per device.

v0:
```python
import jax
import jax.numpy as jnp
from jax import lax
from jax.sharding import PartitionSpec as P

D = 1024
HEADS = 16
HEAD = 64
EXPERTS = 2
SEQ = 1024
MOST = 640


NORM_EPS = 1e-05
SCORE_SCALE = 0.125
MASKED = -1e30


def normalize(values, gain_row, shift_row):
    center = values - jnp.mean(values, axis=-1, keepdims=True)
    spread = jnp.mean(center * center, axis=-1, keepdims=True)
    return center * lax.rsqrt(spread + NORM_EPS) * gain_row + shift_row


def contract_rows(left_side, right_side):
    return lax.dot_general(
        left_side, right_side, (((0,), (0,)), ((), ())), preferred_element_type=jnp.float32
    )


def contract_last(left_side, right_side):
    return lax.dot_general(
        left_side, right_side, (((1,), (1,)), ((), ())), preferred_element_type=jnp.float32
    )


def causal_scores(query_block, key_seq, first_row):
    block_rows = query_block.shape[0]
    length = key_seq.shape[0]
    scores = (
        jnp.einsum("qhd,khd->hqk", query_block, key_seq, preferred_element_type=jnp.float32)
        * SCORE_SCALE
    )
    allowed = jnp.arange(length)[None, :] <= (first_row + jnp.arange(block_rows))[:, None]
    return jnp.where(allowed[None], scores, MASKED)


def block_layout(row_count):
    block_rows = min(512, SEQ)
    return (block_rows, SEQ // block_rows, row_count // SEQ)


def attention_forward(query, keys_low, values_low):
    row_count = query.shape[0]
    block_rows, per_seq, seq_count = block_layout(row_count)
    query_blocks = query.reshape(seq_count * per_seq, block_rows, HEADS, HEAD)
    key_seqs = keys_low.reshape(seq_count, SEQ, HEADS, HEAD)
    value_seqs = values_low.reshape(seq_count, SEQ, HEADS, HEAD)

    def one_block(position):
        seq_index = position // per_seq
        first_row = position % per_seq * block_rows
        query_block = lax.dynamic_index_in_dim(query_blocks, position, 0, keepdims=False)
        key_seq = lax.dynamic_index_in_dim(key_seqs, seq_index, 0, keepdims=False)
        value_seq = lax.dynamic_index_in_dim(value_seqs, seq_index, 0, keepdims=False)
        scores = causal_scores(query_block, key_seq, first_row)
        row_max = jnp.max(scores, axis=-1, keepdims=True)
        weights = jnp.exp(scores - row_max)
        row_total = jnp.sum(weights, axis=-1, keepdims=True)
        weights_low = (weights / row_total).astype(jnp.bfloat16)
        attended = jnp.einsum(
            "hqk,khd->qhd", weights_low, value_seq, preferred_element_type=jnp.float32
        )
        return (attended.astype(jnp.bfloat16), (row_max + jnp.log(row_total))[..., 0])

    attended, log_total = lax.map(one_block, jnp.arange(seq_count * per_seq))
    return (attended.reshape(row_count, HEADS * HEAD), log_total)


def attention_backward(query, keys_low, values_low, log_total, grad_low):
    row_count = query.shape[0]
    block_rows, per_seq, seq_count = block_layout(row_count)
    query_blocks = query.reshape(seq_count * per_seq, block_rows, HEADS, HEAD)
    grad_blocks = grad_low.reshape(seq_count * per_seq, block_rows, HEADS, HEAD)
    key_seqs = keys_low.reshape(seq_count, SEQ, HEADS, HEAD)
    value_seqs = values_low.reshape(seq_count, SEQ, HEADS, HEAD)

    def one_block(position):
        seq_index = position // per_seq
        first_row = position % per_seq * block_rows
        query_block = lax.dynamic_index_in_dim(query_blocks, position, 0, keepdims=False)
        grad_block = lax.dynamic_index_in_dim(grad_blocks, position, 0, keepdims=False)
        log_block = lax.dynamic_index_in_dim(log_total, position, 0, keepdims=False)
        key_seq = lax.dynamic_index_in_dim(key_seqs, seq_index, 0, keepdims=False)
        value_seq = lax.dynamic_index_in_dim(value_seqs, seq_index, 0, keepdims=False)
        scores = causal_scores(query_block, key_seq, first_row)
        weights = jnp.exp(scores - log_block[..., None])
        grad_weights = jnp.einsum(
            "qhd,khd->hqk", grad_block, value_seq, preferred_element_type=jnp.float32
        )
        row_inner = jnp.sum(weights * grad_weights, axis=-1, keepdims=True)
        grad_scores = (weights * (grad_weights - row_inner)).astype(jnp.bfloat16)
        grad_query = (
            jnp.einsum("hqk,khd->qhd", grad_scores, key_seq, preferred_element_type=jnp.float32)
            * SCORE_SCALE
        )
        grad_key = (
            jnp.einsum("hqk,qhd->khd", grad_scores, query_block, preferred_element_type=jnp.float32)
            * SCORE_SCALE
        )
        grad_value = jnp.einsum(
            "hqk,qhd->khd",
            weights.astype(jnp.bfloat16),
            grad_block,
            preferred_element_type=jnp.float32,
        )
        return (grad_query, grad_key, grad_value)

    grad_query, grad_key, grad_value = lax.map(one_block, jnp.arange(seq_count * per_seq))
    grad_query = grad_query.reshape(row_count, D)
    grad_key = grad_key.reshape(seq_count, per_seq, SEQ, D).sum(axis=1).reshape(row_count, D)
    grad_value = grad_value.reshape(seq_count, per_seq, SEQ, D).sum(axis=1).reshape(row_count, D)
    return (grad_query, grad_key, grad_value)


def shards(
    tokens,
    norm_gain,
    norm_bias,
    w_qkv,
    attn_bias,
    w_attn_out,
    expert_in,
    expert_in_bias,
    expert_out,
    expert_out_bias,
    expert_ids,
    running_load,
    cotangent,
):
    qkv_full, attn_out_full, gain_full, shift_full, bias_full = (
        lax.all_gather(w_qkv, ("dp", "fsdp"), axis=0, tiled=True),
        lax.all_gather(w_attn_out, ("dp", "fsdp"), axis=0, tiled=True),
        lax.all_gather(norm_gain, ("dp", "fsdp"), axis=1, tiled=True),
        lax.all_gather(norm_bias, ("dp", "fsdp"), axis=1, tiled=True),
        lax.all_gather(attn_bias, ("dp", "fsdp"), axis=1, tiled=True),
    )
    norm_gains = gain_full.astype(jnp.float32)
    shifts = shift_full.astype(jnp.float32)
    biases = bias_full.astype(jnp.float32)
    inputs = tokens.astype(jnp.float32)
    normed_one = normalize(inputs, norm_gains[0], shifts[0]).astype(jnp.bfloat16)
    projected = jnp.dot(normed_one, qkv_full, preferred_element_type=jnp.float32)
    query = (projected[:, :D] + biases[0]).astype(jnp.bfloat16)
    keys_low = projected[:, D : 2 * D].astype(jnp.bfloat16)
    values_low = (projected[:, 2 * D :] + biases[1]).astype(jnp.bfloat16)
    attended, log_total = attention_forward(query, keys_low, values_low)
    residual = inputs + (
        jnp.dot(attended, attn_out_full, preferred_element_type=jnp.float32) + biases[2]
    )
    normed_two = normalize(residual, norm_gains[1], shifts[1]).astype(jnp.bfloat16)
    token_experts = expert_ids[:, 0]
    matches = token_experts[:, None] == jnp.arange(EXPERTS)[None, :]
    local_counts = jnp.sum(matches.astype(jnp.int32), axis=0)
    offsets = jnp.cumsum(local_counts) - local_counts
    grouped = jnp.argsort(token_experts, stable=True)
    grouped = jnp.concatenate([grouped, jnp.zeros((MOST,), jnp.int32)])
    slot_ids = jnp.arange(MOST)
    expert_sum = jnp.zeros_like(inputs)
    kept_forward = []
    kept_weights = []
    for expert in range(EXPERTS):
        in_full, out_full, in_bias_full, out_bias_full = (
            lax.all_gather(expert_in[expert], ("dp", "fsdp"), axis=0, tiled=True),
            lax.all_gather(expert_out[expert], ("dp", "fsdp"), axis=0, tiled=True),
            lax.all_gather(expert_in_bias[expert], ("dp", "fsdp"), axis=0, tiled=True),
            lax.all_gather(expert_out_bias[expert], ("dp", "fsdp"), axis=0, tiled=True),
        )
        members = lax.dynamic_slice_in_dim(grouped, offsets[expert], MOST)
        live_slots = (slot_ids < local_counts[expert])[:, None]
        picked = jnp.take(normed_two, members, axis=0)
        hidden_pre = jnp.dot(
            picked, in_full, preferred_element_type=jnp.float32
        ) + in_bias_full.astype(jnp.float32)
        hidden_low = jax.nn.gelu(hidden_pre).astype(jnp.bfloat16)
        produced = jnp.dot(
            hidden_low, out_full, preferred_element_type=jnp.float32
        ) + out_bias_full.astype(jnp.float32)
        expert_sum = expert_sum.at[members].add(jnp.where(live_slots, produced, 0.0))
        kept_forward.append((members, live_slots, picked, hidden_pre, hidden_low))
        kept_weights.append(None)
    block_out = (residual + expert_sum).astype(jnp.bfloat16)
    count_total = lax.psum(local_counts.astype(jnp.float32), ("dp", "fsdp"))
    expert_counts = count_total.astype(jnp.int32)
    token_total = tokens.shape[0] * lax.axis_size(("dp", "fsdp"))
    expert_load = 0.9 * running_load + 0.1 * (count_total * EXPERTS / token_total)
    grad_output = cotangent.astype(jnp.float32)
    grad_normed_two = jnp.zeros_like(inputs)
    expert_grads = []
    for expert in range(EXPERTS):
        in_full, out_full = (
            lax.all_gather(expert_in[expert], ("dp", "fsdp"), axis=0, tiled=True),
            lax.all_gather(expert_out[expert], ("dp", "fsdp"), axis=0, tiled=True),
        )
        members, live_slots, picked, hidden_pre, hidden_low = kept_forward[expert]
        grad_rows = jnp.where(
            live_slots, jnp.take(cotangent, members, axis=0), jnp.zeros((), jnp.bfloat16)
        )
        grad_hidden = contract_last(grad_rows, out_full)
        gelu_value, gelu_back = jax.vjp(jax.nn.gelu, hidden_pre)
        grad_pre = gelu_back(grad_hidden)[0].astype(jnp.bfloat16)
        grad_normed_two = grad_normed_two.at[members].add(
            jnp.where(live_slots, contract_last(grad_pre, in_full), 0.0)
        )
        grad_terms = (
            contract_rows(picked, grad_pre),
            contract_rows(hidden_low, grad_rows),
            jnp.sum(grad_pre.astype(jnp.float32), axis=0),
            jnp.sum(grad_rows.astype(jnp.float32), axis=0),
        )
        expert_grads.append(
            (
                lax.psum_scatter(grad_terms[0], ("dp", "fsdp"), scatter_dimension=0, tiled=True),
                lax.psum_scatter(grad_terms[1], ("dp", "fsdp"), scatter_dimension=0, tiled=True),
                lax.psum_scatter(grad_terms[2], ("dp", "fsdp"), scatter_dimension=0, tiled=True),
                lax.psum_scatter(grad_terms[3], ("dp", "fsdp"), scatter_dimension=0, tiled=True),
            )
        )
    stacked = tuple(
        (jnp.stack([member_grads[column] for member_grads in expert_grads]) for column in range(4))
    )
    in_grad, out_grad, in_bias_grad, out_bias_grad = stacked
    norm_value, norm_back = jax.vjp(normalize, residual, norm_gains[1], shifts[1])
    grad_residual_norm, grad_gain_two, grad_shift_two = norm_back(grad_normed_two)
    grad_residual = grad_output + grad_residual_norm
    grad_branch = grad_residual.astype(jnp.bfloat16)
    qkv_full, attn_out_full = (
        lax.all_gather(w_qkv, ("dp", "fsdp"), axis=0, tiled=True),
        lax.all_gather(w_attn_out, ("dp", "fsdp"), axis=0, tiled=True),
    )
    grad_attn_out = contract_rows(attended, grad_branch)
    grad_attended = contract_last(grad_branch, attn_out_full).astype(jnp.bfloat16)
    grad_query, grad_key, grad_value = attention_backward(
        query, keys_low, values_low, log_total, grad_attended
    )
    grad_projected = jnp.concatenate(
        [
            grad_query.astype(jnp.bfloat16),
            grad_key.astype(jnp.bfloat16),
            grad_value.astype(jnp.bfloat16),
        ],
        axis=1,
    )
    grad_qkv = contract_rows(normed_one, grad_projected)
    grad_normed_one = contract_last(grad_projected, qkv_full)
    norm_value, norm_back = jax.vjp(normalize, inputs, norm_gains[0], shifts[0])
    grad_inputs_norm, grad_gain_one, grad_shift_one = norm_back(grad_normed_one)
    input_grad = grad_residual + grad_inputs_norm
    grad_biases = jnp.stack(
        [
            jnp.sum(grad_projected[:, :D].astype(jnp.float32), axis=0),
            jnp.sum(grad_projected[:, 2 * D :].astype(jnp.float32), axis=0),
            jnp.sum(grad_branch.astype(jnp.float32), axis=0),
        ]
    )
    qkv_sum, attn_out_sum, gain_sum, shift_sum, bias_sum = (
        lax.psum_scatter(grad_qkv, ("dp", "fsdp"), scatter_dimension=0, tiled=True),
        lax.psum_scatter(grad_attn_out, ("dp", "fsdp"), scatter_dimension=0, tiled=True),
        lax.psum_scatter(
            jnp.stack([grad_gain_one, grad_gain_two]),
            ("dp", "fsdp"),
            scatter_dimension=1,
            tiled=True,
        ),
        lax.psum_scatter(
            jnp.stack([grad_shift_one, grad_shift_two]),
            ("dp", "fsdp"),
            scatter_dimension=1,
            tiled=True,
        ),
        lax.psum_scatter(grad_biases, ("dp", "fsdp"), scatter_dimension=1, tiled=True),
    )
    return (
        block_out,
        input_grad,
        gain_sum,
        shift_sum,
        qkv_sum,
        bias_sum,
        attn_out_sum,
        in_grad,
        in_bias_grad,
        out_grad,
        out_bias_grad,
        expert_counts,
        expert_load,
    )


def solution(mesh):
    placed = (
        P(("dp", "fsdp"), None),
        P(None, ("dp", "fsdp")),
        P(None, ("dp", "fsdp")),
        P(("dp", "fsdp"), None),
        P(None, ("dp", "fsdp")),
        P(("dp", "fsdp"), None),
        P(None, ("dp", "fsdp"), None),
        P(None, ("dp", "fsdp")),
        P(None, ("dp", "fsdp"), None),
        P(None, ("dp", "fsdp")),
        P(("dp", "fsdp"), None),
        P(),
        P(("dp", "fsdp"), None),
    )
    return jax.shard_map(
        shards,
        mesh=mesh,
        in_specs=placed,
        out_specs=(
            P(("dp", "fsdp"), None),
            P(("dp", "fsdp"), None),
            P(None, ("dp", "fsdp")),
            P(None, ("dp", "fsdp")),
            P(("dp", "fsdp"), None),
            P(None, ("dp", "fsdp")),
            P(("dp", "fsdp"), None),
            P(None, ("dp", "fsdp"), None),
            P(None, ("dp", "fsdp")),
            P(None, ("dp", "fsdp"), None),
            P(None, ("dp", "fsdp")),
            P(),
            P(),
        ),
        check_vma=False,
    )
```

profile of v0, /device:TPU:0, one launch (start us, length us, event | category | flops | bytes accessed | tf_op | source)
XLA Modules:
  0.0 2242.1 jit_solution(5193095624714337481)
XLA Ops:
  29.8 43.3 %all-gather.5 = bf16[1,4096]{1,0:T(2,128)(2,1)S(1)} all-gather(bf16[1,128]{1,0:T(2,128)(2,1)S(1)} %get-tuple-element.468), channel_id=7, replica_groups=mesh['dp'=4,'fsdp'=8] {'dp','fsdp'}, dimensions={1}, use_global_device_ids=true | all-gather | bytes 8448 | tf_op jit(solution)/shard_map/all_gather | solution.py:176
  73.8 36.5 %all-gather.1 = bf16[1,4096]{1,0:T(2,128)(2,1)S(1)} all-gather(bf16[1,128]{1,0:T(2,128)(2,1)S(1)} %get-tuple-element.469), channel_id=3, replica_groups=mesh['dp'=4,'fsdp'=8] {'dp','fsdp'}, dimensions={1}, use_global_device_ids=true | all-gather | bytes 8448 | tf_op jit(solution)/shard_map/all_gather | solution.py:176
  110.9 37.9 %all-gather.8 = bf16[32,32,2]{1,2,0:T(2,128)(2,1)S(1)} all-gather(bf16[1,32,2]{1,2,0:T(2,128)(2,1)} %bitcast.277), channel_id=1, replica_groups=mesh['dp'=4,'fsdp'=8] {'dp','fsdp'}, dimensions={0}, use_global_device_ids=true | all-gather | bytes 4224 | tf_op jit(solution)/shard_map/all_gather | solution.py:144
  149.5 36.9 %all-gather.9 = bf16[32,32,2]{1,2,0:T(2,128)(2,1)S(1)} all-gather(bf16[1,32,2]{1,2,0:T(2,128)(2,1)} %bitcast.278), channel_id=1, replica_groups=mesh['dp'=4,'fsdp'=8] {'dp','fsdp'}, dimensions={0}, use_global_device_ids=true | all-gather | bytes 4224 | tf_op jit(solution)/shard_map/all_gather | solution.py:145
  187.1 38.6 %all-gather.10 = bf16[32,32,3]{1,2,0:T(4,128)(2,1)S(1)} all-gather(bf16[1,32,3]{1,2,0:T(4,128)(2,1)} %bitcast.276), channel_id=1, replica_groups=mesh['dp'=4,'fsdp'=8] {'dp','fsdp'}, dimensions={0}, use_global_device_ids=true | all-gather | bytes 6336 | tf_op jit(solution)/shard_map/all_gather | solution.py:146
  272.7 102.1 %while.30 = (s32[]{:T(128)}, bf16[2,512,16,64]{1,3,2,0:T(8,128)(2,1)S(1)}, f32[2,16,512]{2,1,0:T(8,128)S(1)}, s32[2]{0:T(128)S(1)}, bf16[2,512,16,64]{1,3,2,0:T(...) while((s32[]{:T(128)}, ...), condition=%wide.region_5.6_spmd, body=%wide.region_2.5_spmd.sunk | while | flops 2249187840 | bytes 109318432 | solution.py:76
  537.6 221.2 %while.31 = (s32[]{:T(128)}, bf16[2,512,16,64]{1,3,2,0:T(8,128)(2,1)}, f32[2,1024,16,64]{1,3,2,0:T(8,128)}, f32[2,1024,16,64]{1,3,2,0:T(8,128)}, s32[2]{0:T(128)...) while((s32[]{:T(128)}, ...), condition=%wide.region_19.21_spmd, body=%wide.region_17.20_spmd.sunk | while | flops 5496627712 | bytes 342069568 | solution.py:119
  542.3 17.5 fusion.189
  559.8 17.0 bitcast_dynamic-update-slice_fusion.11
  576.8 25.9 %multiply_reduce_fusion.5 = (f32[16,512]{1,0:T(8,128)S(1)}, f32[16,512,1024]{2,1,0:T(8,128)}) fusion(f32[16,512,1024]{2,1,0:T(8,128)} %fusion.189, f32[16,512]{1,0:T(8,128)S(1)} %dynamic-slice_bitcast_fusion.6, pred[512,1024]{1,0:T(8,128)(4,1)S(1)} %iota_compare_fusion.7, bf16[1,1024,16,64]{1,3,2,0:T(8,128)(2,1)} %get-tuple-element.666, ...), kind=kOutput, calls=%fused_computation.29.clone.1 | convolution fusion | flops 1115676672 | bytes 70844416 | tf_op jit(solution)/shard_map/while/body/eval_jaxpr/qhd,khd->hqk/dot_general | solution.py:98
  602.8 27.7 %multiply_convert_fusion.8 = bf16[16,512,1024]{2,1,0:T(8,128)(2,1)} fusion(f32[16,512,1024]{2,1,0:T(8,128)} %get-tuple-element.594, f32[16,512,1024]{2,1,0:T(8,128)} %fusion.189, f32[16,512]{1,0:T(8,128)S(1)} %get-tuple-element.595, f32[16,512]{1,0:T(8,128)S(1)} %dynamic-slice_bitcast_fusion.6, pred[512,1024]{1,0:T(8,128)(4,1)S(1)} %iota_compare_fusion.7), kind=kLoop, calls=%fused_computation.28.clone.1 | loop fusion | flops 50331648 | bytes 84475904 | tf_op jit(solution)/shard_map/while/body/eval_jaxpr/convert_element_type | solution.py:102
  652.6 17.5 fusion.189
  670.2 17.1 bitcast_dynamic-update-slice_fusion.11
  687.3 25.9 %multiply_reduce_fusion.5 = (f32[16,512]{1,0:T(8,128)S(1)}, f32[16,512,1024]{2,1,0:T(8,128)}) fusion(f32[16,512,1024]{2,1,0:T(8,128)} %fusion.189, f32[16,512]{1,0:T(8,128)S(1)} %dynamic-slice_bitcast_fusion.6, pred[512,1024]{1,0:T(8,128)(4,1)S(1)} %iota_compare_fusion.7, bf16[1,1024,16,64]{1,3,2,0:T(8,128)(2,1)} %get-tuple-element.666, ...), kind=kOutput, calls=%fused_computation.29.clone.1 | convolution fusion | flops 1115676672 | bytes 70844416 | tf_op jit(solution)/shard_map/while/body/eval_jaxpr/qhd,khd->hqk/dot_general | solution.py:98
  713.2 27.7 %multiply_convert_fusion.8 = bf16[16,512,1024]{2,1,0:T(8,128)(2,1)} fusion(f32[16,512,1024]{2,1,0:T(8,128)} %get-tuple-element.594, f32[16,512,1024]{2,1,0:T(8,128)} %fusion.189, f32[16,512]{1,0:T(8,128)S(1)} %get-tuple-element.595, f32[16,512]{1,0:T(8,128)S(1)} %dynamic-slice_bitcast_fusion.6, pred[512,1024]{1,0:T(8,128)(4,1)S(1)} %iota_compare_fusion.7), kind=kLoop, calls=%fused_computation.28.clone.1 | loop fusion | flops 50331648 | bytes 84475904 | tf_op jit(solution)/shard_map/while/body/eval_jaxpr/convert_element_type | solution.py:102
  885.4 37.1 %all-reduce.8 = (bf16[1024]{0:T(1024)(128)(2,1)S(1)}, bf16[1024]{0:T(1024)(128)(2,1)S(1)}) all-reduce(bf16[1024]{0:T(1024)(128)(2,1)S(1)} %dynamic-update-slice, bf16[1024]{0:T(1024)(128)(2,1)S(1)} %dynamic-update-slice.1), channel_id=5, replica_groups=mesh['dp'=4,'fsdp'=8] {'dp','fsdp'}, use_global_device_ids=true, to_apply=%add.1 | all-reduce | flops 2048 | bytes 8192
  1002.0 42.0 %all-reduce.7 = (f32[4096]{0:T(1024)S(1)}, f32[4096]{0:T(1024)S(1)}, f32[1024]{0:T(1024)S(1)}, f32[1024]{0:T(1024)S(1)}, f32[2]{0:T(128)S(1)}) all-reduce(f32[4096]{0:T(1024)S(1)} %copy-done.56, f32[4096]{0:T(1024)S(1)} %copy-done.55, f32[1024]{0:T(1024)S(1)} %get-tuple-element.482, ...), channel_id=18, replica_groups=mesh['dp'=4,'fsdp'=8] {'dp','fsdp'}, use_global_device_ids=true, to_apply=%region_41.43.clone | all-reduce | flops 10242 | bytes 81936
  1058.4 130.8 %reduce-scatter.32.cloned.1.call-done = f32[32,3]{1,0:T(8,128)} async-done(((f32[1024,3]{1,0:T(8,128)}), f32[32,3]{1,0:T(8,128)}) %reduce-scatter.32.cloned.1.call-update) | async-done | bytes 400
  1190.6 179.8 %reduce-scatter.24.cloned.1.call-done = f32[128,1024]{1,0:T(8,128)} async-done(((f32[4096,1024]{1,0:T(8,128)}), f32[128,1024]{1,0:T(8,128)}) %reduce-scatter.24.cloned.1.call-update) | async-done | bytes 524304 | tf_op jit(solution)/shard_map/reduce_scatter | solution.py:224
  1370.4 186.9 %reduce-scatter.26.cloned.1.call-done = f32[128,1024]{1,0:T(8,128)} async-done(((f32[4096,1024]{1,0:T(8,128)}), f32[128,1024]{1,0:T(8,128)}) %reduce-scatter.26.cloned.1.call-update) | async-done | bytes 524304 | tf_op jit(solution)/shard_map/reduce_scatter | solution.py:224
  1559.6 184.5 %reduce-scatter.20.cloned.1.call-done = f32[32,4096]{1,0:T(8,128)} async-done(((f32[1024,4096]{1,0:T(8,128)}), f32[32,4096]{1,0:T(8,128)}) %reduce-scatter.20.cloned.1.call-update) | async-done | bytes 524304 | tf_op jit(solution)/shard_map/reduce_scatter | solution.py:223
  1744.1 186.9 %reduce-scatter.22.cloned.1.call-done = f32[32,4096]{1,0:T(8,128)} async-done(((f32[1024,4096]{1,0:T(8,128)}), f32[32,4096]{1,0:T(8,128)}) %reduce-scatter.22.cloned.1.call-update) | async-done | bytes 524304 | tf_op jit(solution)/shard_map/reduce_scatter | solution.py:223
  1933.2 143.0 %reduce-scatter.18.cloned.1.call-done = f32[32,1024]{1,0:T(8,128)} async-done(((f32[1024,1024]{1,0:T(8,128)}), f32[32,1024]{1,0:T(8,128)}) %reduce-scatter.18.cloned.1.call-update) | async-done | bytes 131088 | tf_op jit(solution)/shard_map/reduce_scatter | solution.py:268
  2076.2 159.1 %reduce-scatter.16.cloned.1.call-done = f32[32,3072]{1,0:T(8,128)} async-done(((f32[1024,3072]{1,0:T(8,128)}), f32[32,3072]{1,0:T(8,128)}) %reduce-scatter.16.cloned.1.call-update) | async-done | bytes 393232 | tf_op jit(solution)/shard_map/reduce_scatter | solution.py:267
  (332 shorter events, 589.1 us)
Async XLA Ops:
  7.2 219.1 %copy-start.1 = (bf16[1024,1024]{1,0:T(8,128)(2,1)S(1)}, bf16[1024,1024]{1,0:T(8,128)(2,1)}, u32[]{:S(2)}) copy-start(bf16[1024,1024]{1,0:T(8,128)(2,1)} %param.31) | copy-start | bytes 6291460
  7.2 232.6 %all-gather.18.cloned.1.call-start = ((), (), s32[]{:S(2)}) async-start(), calls=%async_computation.9 | async-start | bytes 6488064 | tf_op jit(solution)/shard_map/all_gather | solution.py:142
  7.9 374.1 %all-gather.20.cloned.1.call-start = ((), (), s32[]{:S(2)}) async-start(), calls=%async_computation.10 | async-start | bytes 2162688 | tf_op jit(solution)/shard_map/all_gather | solution.py:143
  8.7 391.5 %all-gather.22.cloned.1.call-start = ((), (), s32[]{:S(2)}) async-start(), calls=%async_computation.17 | async-start | bytes 8650752 | tf_op jit(solution)/shard_map/all_gather | solution.py:174
  10.6 400.4 %all-gather.24.cloned.1.call-start = ((), (), s32[]{:S(2)}) async-start(), calls=%async_computation.18 | async-start | bytes 8650752 | tf_op jit(solution)/shard_map/all_gather | solution.py:175
  12.6 440.7 %all-gather.26.cloned.1.call-start = ((), (), s32[]{:S(2)}) async-start(), calls=%async_computation.19 | async-start | bytes 8650752 | tf_op jit(solution)/shard_map/all_gather | solution.py:174
  13.1 452.5 %all-gather.28.cloned.1.call-start = ((), (), s32[]{:S(2)}) async-start(), calls=%async_computation.20 | async-start | bytes 8650752 | tf_op jit(solution)/shard_map/all_gather | solution.py:175
  13.7 1032.2 %reduce-scatter.30.cloned.1.call-start = ((), (), s32[]{:S(2)}) async-start(), calls=%async_computation.22 | async-start | bytes 540672
  29.3 203.1 %copy-start.41 = (s32[1024]{0:T(1024)}, s32[1024]{0:T(1024)S(1)}, u32[]{:S(2)}) copy-start(s32[1024]{0:T(1024)S(1)} %pad_clamp_fusion) | copy-start | bytes 12292
  29.8 202.6 %copy-start.39 = (s32[1024]{0:T(1024)}, s32[1024]{0:T(1024)S(1)}, u32[]{:S(2)}) copy-start(s32[1024]{0:T(1024)S(1)} %pad_clamp_fusion.1) | copy-start | bytes 12292
  149.5 90.3 %copy-start.33 = (f32[1,1024]{1,0:T(1,128)}, f32[1,1024]{1,0:T(1,128)S(1)}, u32[]{:S(2)}) copy-start(f32[1,1024]{1,0:T(1,128)S(1)} %get-tuple-element.457) | copy-start | bytes 12292
  187.1 52.8 %copy-start.61 = (f32[1,1024]{1,0:T(1,128)}, f32[1,1024]{1,0:T(1,128)S(1)}, u32[]{:S(2)}) copy-start(f32[1,1024]{1,0:T(1,128)S(1)} %get-tuple-element.459) | copy-start | bytes 12292
  396.6 56.6 %copy-start.20 = (bf16[640,1024]{1,0:T(8,128)(2,1)}, bf16[640,1024]{1,0:T(8,128)(2,1)S(1)}, u32[]{:S(2)}) copy-start(bf16[640,1024]{1,0:T(8,128)(2,1)S(1)} %gather_fusion.1) | copy-start | bytes 3932164
  440.0 13.2 copy-start.26
  453.2 12.4 copy-start.19
  792.8 264.2 %reduce-scatter.28.cloned.1.call-start = ((), (), s32[]{:S(2)}) async-start(), calls=%async_computation.21 | async-start | bytes 540672
  805.5 383.7 %reduce-scatter.32.cloned.1.call-start = ((), (), s32[]{:S(2)}) async-start(), calls=%async_computation.23 | async-start | bytes 540672
  806.7 563.7 %reduce-scatter.24.cloned.1.call-start = ((), (), s32[]{:S(2)}) async-start(), calls=%async_computation.15 | async-start | bytes 17301504 | tf_op jit(solution)/shard_map/reduce_scatter | solution.py:224
  821.3 736.0 %reduce-scatter.26.cloned.1.call-start = ((), (), s32[]{:S(2)}) async-start(), calls=%async_computation.16 | async-start | bytes 17301504 | tf_op jit(solution)/shard_map/reduce_scatter | solution.py:224
  837.0 907.1 %reduce-scatter.20.cloned.1.call-start = ((), (), s32[]{:S(2)}) async-start(), calls=%async_computation.13 | async-start | bytes 17301504 | tf_op jit(solution)/shard_map/reduce_scatter | solution.py:223
  850.0 1080.9 %reduce-scatter.22.cloned.1.call-start = ((), (), s32[]{:S(2)}) async-start(), calls=%async_computation.14 | async-start | bytes 17301504 | tf_op jit(solution)/shard_map/reduce_scatter | solution.py:223
  862.6 1213.6 %reduce-scatter.18.cloned.1.call-start = ((), (), s32[]{:S(2)}) async-start(), calls=%async_computation.12 | async-start | bytes 4325376 | tf_op jit(solution)/shard_map/reduce_scatter | solution.py:268
  869.3 1366.0 %reduce-scatter.16.cloned.1.call-start = ((), (), s32[]{:S(2)}) async-start(), calls=%async_computation.11 | async-start | bytes 12976128 | tf_op jit(solution)/shard_map/reduce_scatter | solution.py:267
  996.6 48.8 %copy-start.66 = (f32[2]{0:T(128)S(1)}, f32[2]{0:T(128)}, u32[]{:S(2)}) copy-start(f32[2]{0:T(128)} %param.30) | copy-start | bytes 28
  (60 other events, 301.4 us)
Sparse Core Ops, SparseCore 0:
  10.9 73.7 all-gather.17
  87.5 54.9 all-gather.19
  145.3 76.4 all-gather.21
  225.1 76.1 all-gather.23
  304.6 76.0 all-gather.25
  384.0 76.0 all-gather.27
  792.9 130.9 reduce-scatter.29
  926.8 130.1 reduce-scatter.27
  1059.3 129.8 reduce-scatter.31
  1191.5 178.8 reduce-scatter.23
  1372.8 184.4 reduce-scatter.25
  1559.6 184.4 reduce-scatter.19
  1746.5 184.4 reduce-scatter.21
  1933.8 142.4 reduce-scatter.17
  2083.7 151.6 reduce-scatter.15
where the time goes:
time: 2250 us; the launch traced here: 2240 us
  waiting for transfers between devices  1180 us (52%)
  matrix products  421 us (19%)
  blocking collectives  272 us (12%)
  other arithmetic  213 us (9%)
  local copies, waits for them, and re-layouts  118 us (5%)
    reduce_scatter x2, waiting for transfers between devices, shards(): lax.psum_scatter(grad_terms[0], ('dp', 'fsdp'), scatter_dimension=0, tile...  371 us
    reduce_scatter x2, waiting for transfers between devices, shards(): lax.psum_scatter(grad_terms[1], ('dp', 'fsdp'), scatter_dimension=0, tile...  367 us
    reduce_scatter x1, waiting for transfers between devices, shards(): lax.psum_scatter(grad_qkv, ('dp', 'fsdp'), scatter_dimension=0, tiled=True)  159 us
    unnamed x18, waiting for transfers between devices  143 us
    reduce_scatter x1, waiting for transfers between devices, shards(): lax.psum_scatter(grad_attn_out, ('dp', 'fsdp'), scatter_dimension=0, tile...  143 us
    all_gather x2, blocking collectives, shards(): lax.all_gather(expert_in_bias[expert], ('dp', 'fsdp'), axis=0, tiled=True)  79.8 us
    unnamed x2, blocking collectives  79.1 us
    dot_general x6, matrix products, contract_rows(): lax.dot_general(left_side, right_side, (((0,), (0,)), ((), ())), preferre...  75.8 us
  transfers between devices with their start and end apart: 15, of which 8 were waited for; matrix products, arithmetic and copies ran while one was open for 19% of the time, Pallas kernels for 0%

commit v1 on v0

v1 whole, which is shorter than its diff:
```python
import functools
import math

import jax
import jax.numpy as jnp
from jax import lax
from jax.experimental import pallas as pl
from jax.experimental.pallas import tpu as pltpu
from jax.sharding import Mesh, PartitionSpec as P

BF16 = jnp.bfloat16
F32 = jnp.float32
MESH_ID = pl.DeviceIdType.MESH

HEAD = 64
SEQ = 1024
MOST = 640
EXPERTS = 2
CHUNKS = 2
NORM_EPS = 1e-05
SCORE_SCALE = 0.125
SCALE_LOG2 = SCORE_SCALE * math.log2(math.e)
MASKED = -1e30
BLOCK = 256
MIB = 1 << 20


def dot(left, right):
    return lax.dot_general(left, right, (((1,), (0,)), ((), ())), preferred_element_type=F32)


def dot_last(left, right):
    return lax.dot_general(left, right, (((1,), (1,)), ((), ())), preferred_element_type=F32)


def row_stats(values):
    center = values - jnp.mean(values, axis=-1, keepdims=True)
    spread = jnp.mean(center * center, axis=-1, keepdims=True)
    inverse = lax.rsqrt(spread + NORM_EPS)
    return center * inverse, inverse


class Place:
    def __init__(self, nz, nx):
        self.nz, self.nx = nz, nx
        self.bits_z, self.bits_x = nz.bit_length() - 1, nx.bit_length() - 1
        self.z, self.xy, self.core = lax.axis_index("dp"), lax.axis_index("xy"), lax.axis_index("core")
        self.flip_z = [(1 - 2 * lax.rem(lax.div(self.z, 2**k), 2)) * 2**k for k in range(self.bits_z)]
        self.flip_x = [(1 - 2 * lax.rem(lax.div(self.xy, 2**k), 2)) * 2**k for k in range(self.bits_x)]

    def step_x(self, k, core=None):
        core = self.core if core is None else core
        return (1 - core) * self.flip_x[k] + core * self.flip_x[self.bits_x - 1 - k]

    def span_x(self, which, core=None):
        return self.xy + sum(self.step_x(k, core) for k in range(self.bits_x) if which >> k & 1)

    def span_z(self, which):
        return self.z + sum(self.flip_z[k] for k in range(self.bits_z) if which >> k & 1)

    def partners(self):
        found = [(self.z + flip, self.xy, self.core) for flip in self.flip_z]
        found += [(self.z, self.xy + flip, self.core) for flip in self.flip_x]
        return found + [(self.z, self.xy, 1 - self.core)]

    def sibling(self):
        return (self.z, self.xy, 1 - self.core)

    def barrier(self):
        semaphore = pltpu.get_barrier_semaphore()
        partners = self.partners()
        for partner in partners:
            pl.semaphore_signal(semaphore, inc=1, device_id=partner, device_id_type=MESH_ID)
        pl.semaphore_wait(semaphore, len(partners))


def remote(src, dst, send, recv, device):
    return pltpu.make_async_remote_copy(
        src_ref=src, dst_ref=dst, send_sem=send, recv_sem=recv, device_id=device, device_id_type=MESH_ID
    )


ALL = slice(None)


class Gather:
    def __init__(self, place, regions, send, recv, to_sibling=None):
        self.place, self.regions, self.send, self.recv = place, regions, send, recv
        self.to_sibling = to_sibling
        self.stages = place.bits_z + place.bits_x + (0 if to_sibling is None else 1)

    def copies(self, piece, stage):
        place, region = self.place, self.regions[piece]
        found = []
        if stage < place.bits_z:
            bit = place.bits_z - 1 - stage
            device = (place.z + place.flip_z[bit], place.xy, place.core)
            for held in range(2**stage):
                found += [(ref, device) for ref in region(place.span_z(held << (bit + 1)), place.xy)]
        elif stage < place.bits_z + place.bits_x:
            step = stage - place.bits_z
            device = (place.z, place.xy + place.step_x(step), place.core)
            for held in range(2**step):
                found += [(ref, device) for ref in region(ALL, place.span_x(held))]
        else:
            found += [(ref, place.sibling()) for ref in self.to_sibling[piece]]
        return [
            remote(ref, ref, self.send.at[piece, stage, i], self.recv.at[piece, stage, i], device)
            for i, (ref, device) in enumerate(found)
        ]

    @property
    def ticks(self):
        return len(self.regions) + self.stages

    def tick(self, now):
        for stage in range(self.stages, -1, -1):
            piece = now - stage
            if not 0 <= piece < len(self.regions):
                continue
            if stage > 0:
                for copy in self.copies(piece, stage - 1):
                    copy.wait()
            if stage < self.stages:
                for copy in self.copies(piece, stage):
                    copy.start()


def gather_semaphores(nz, nx, pieces, width, to_sibling):
    stages = nz.bit_length() - 1 + nx.bit_length() - 1 + int(to_sibling)
    shape = (pieces, stages, width * max(nz // 2, nx // 2, 1))
    return [pltpu.SemaphoreType.DMA(shape), pltpu.SemaphoreType.DMA(shape)]


HBM = pl.BlockSpec(memory_space=pl.ANY)
VMEM = pl.BlockSpec(memory_space=pltpu.VMEM)


def remote_params(collective_id, vmem=32):
    return pltpu.CompilerParams(
        collective_id=collective_id, has_side_effects=True, vmem_limit_bytes=vmem * MIB
    )


def one_hot(slots, count):
    rows = lax.broadcasted_iota(jnp.int32, (count, slots.shape[1]), 0)
    return jnp.where(rows == slots, 1.0, 0.0).astype(BF16)


def pick_rows(picked, slots_ref, values, own_row):
    chosen = one_hot(slots_ref[own_row : own_row + 1, :], picked.shape[0])
    picked[...] = dot(chosen, values).astype(BF16)


def attention_weights(nz, nx, w_qkv, w_out, small, cotangent, slots):
    depth, width = w_qkv.shape
    d = w_out.shape[1]
    parts = width // d
    pieces = parts + 1

    def kernel(
        qkv_ref, out_ref, small_ref, cot_ref, slots_ref, qkv_full, out_full, small_full, grows,
        picked, send, recv, here, pair_send, pair_recv,
    ):
        place = Place(nz, nx)
        z, xy, core = place.z, place.xy, place.core
        own = [
            pltpu.make_async_copy(qkv_ref, qkv_full.at[z, xy, core], here.at[0]),
            pltpu.make_async_copy(out_ref, out_full.at[z, xy, core], here.at[1]),
            pltpu.make_async_copy(small_ref, small_full.at[z, xy, core], here.at[2]),
        ]
        for copy in own:
            copy.start()
        place.barrier()
        for copy in own:
            copy.wait()

        def region(piece):
            if piece == parts:
                return lambda zs, xs: [out_full.at[zs, xs, core]]
            columns = pl.ds(piece * d, d)
            if piece:
                return lambda zs, xs: [qkv_full.at[zs, xs, core, :, columns]]
            return lambda zs, xs: [qkv_full.at[zs, xs, core, :, columns], small_full.at[zs, xs, core]]

        regions = [region(piece) for piece in range(pieces)]
        gather = Gather(place, regions, send, recv, [r(ALL, ALL) for r in regions])
        gather.tick(0)
        pick_rows(picked.at[0], slots_ref, cot_ref[...], 0)
        mine = pltpu.make_async_copy(picked.at[0], grows.at[0], here.at[3])
        mine.start()
        gather.tick(1)
        pick_rows(picked.at[1], slots_ref, cot_ref[...], 1)
        theirs = remote(picked.at[1], grows.at[1], pair_send, pair_recv, place.sibling())
        theirs.start()
        for now in range(2, gather.ticks):
            gather.tick(now)
        mine.wait()
        theirs.wait()

    return pl.pallas_call(
        kernel,
        out_shape=[
            jax.ShapeDtypeStruct((nz, nx, 2, depth, width), BF16),
            jax.ShapeDtypeStruct((nz, nx, 2, depth, d), BF16),
            jax.ShapeDtypeStruct((nz, nx, 2) + small.shape, BF16),
            jax.ShapeDtypeStruct((2, MOST, d), BF16),
        ],
        in_specs=[HBM, HBM, HBM, VMEM, VMEM],
        out_specs=[HBM] * 4,
        scratch_shapes=[
            pltpu.VMEM((2, MOST, d), BF16),
            *gather_semaphores(nz, nx, pieces, 2, True),
            pltpu.SemaphoreType.DMA((4,)),
            pltpu.SemaphoreType.DMA,
            pltpu.SemaphoreType.DMA,
        ],
        compiler_params=remote_params(1),
        name="attention_weights",
    )(w_qkv, w_out, small, cotangent, slots)


class Reduce:
    def __init__(self, place, pieces, pair_first, send, recv, here):
        self.place, self.pieces, self.pair_first = place, pieces, pair_first
        self.send, self.recv, self.here = send, recv, here
        self.stages = place.bits_z + place.bits_x + 1

    def plan(self, piece, stage):
        place = self.place
        source, buffers, target = self.pieces[piece]
        acc, landing = buffers[0], buffers[1:]
        nx, nz, bits_x = place.nx, place.nz, place.bits_x
        far, near, sums = [], [], []
        slot = stage
        if self.pair_first:
            if stage == 0:
                for r in range(nx):
                    far.append((source(ALL, place.span_x(r, 1 - place.core), 1 - place.core), landing[0].at[r], place.sibling()))
                    near.append((source(ALL, place.span_x(r), place.core), acc.at[r]))
                return self.copies(piece, stage, far, near), [(acc.at[r], landing[0].at[r]) for r in range(nx)]
            stage -= 1
        elif stage == self.stages - 1:
            mine = acc.at[0, place.z]
            far.append((mine.at[1 - place.core], target.at[place.core], place.sibling()))
            near.append((mine.at[place.core], target.at[place.core]))
            return self.copies(piece, slot, far, near), []
        if stage < bits_x:
            k = bits_x - 1 - stage
            device = (place.z, place.xy + place.step_x(k), place.core)
            if stage == 0 and not self.pair_first:
                for j in range(2**k):
                    far.append((source(ALL, place.span_x(2**k + j), place.core), landing[slot].at[j], device))
                    near.append((source(ALL, place.span_x(j), place.core), acc.at[j]))
            else:
                far.append((acc.at[pl.ds(2**k, 2**k)], landing[slot], device))
            sums = [(acc.at[j], landing[slot].at[j]) for j in range(2**k)]
        else:
            bit = stage - bits_x
            device = (place.z + place.flip_z[bit], place.xy, place.core)
            for s in range(2 ** (place.bits_z - 1 - bit)):
                upper = s << (bit + 1)
                far.append((acc.at[0, place.span_z(upper + 2**bit)], landing[slot].at[s], device))
                sums.append((acc.at[0, place.span_z(upper)], landing[slot].at[s]))
        return self.copies(piece, slot, far, near), sums

    def copies(self, piece, slot, far, near):
        made = [
            remote(src, dst, self.send.at[piece, slot, i], self.recv.at[piece, slot, i], device)
            for i, (src, dst, device) in enumerate(far)
        ]
        return made + [
            pltpu.make_async_copy(src, dst, self.here.at[piece, slot, i]) for i, (src, dst) in enumerate(near)
        ]

    def begin(self, piece, stage):
        for copy in self.plan(piece, stage)[0]:
            copy.start()

    def finish(self, piece, stage):
        copies, sums = self.plan(piece, stage)
        for copy in copies:
            copy.wait()
        for total, landed in sums:
            if len(total.shape) > 3:
                @pl.loop(0, total.shape[0])
                def _(i, total=total, landed=landed):
                    total[i] = (total[i].astype(F32) + landed[i].astype(F32)).astype(BF16)
            else:
                total[...] = (total[...].astype(F32) + landed[...].astype(F32)).astype(BF16)
        if self.pair_first and stage == self.stages - 1:
            source, buffers, target = self.pieces[piece]
            last = pltpu.make_async_copy(buffers[0].at[0, self.place.z], target, self.here.at[piece, stage, 0])
            last.start()
            last.wait()

    @property
    def ticks(self):
        return len(self.pieces) + self.stages

    def tick(self, now):
        for stage in range(self.stages, -1, -1):
            piece = now - stage
            if not 0 <= piece < len(self.pieces):
                continue
            if stage > 0:
                self.finish(piece, stage - 1)
            if stage < self.stages:
                self.begin(piece, stage)


def reduce_buffers(nz, nx, tail, pair_first):
    bits_z, bits_x = nz.bit_length() - 1, nx.bit_length() - 1
    held = nx if pair_first else nx // 2
    shapes = [(held, nz) + tail]
    if pair_first:
        shapes.append((nx, nz) + tail)
    shapes += [(2**k, nz) + tail for k in reversed(range(bits_x))]
    shapes += [(2 ** (bits_z - 1 - bit),) + tail for bit in range(bits_z)]
    return [pltpu.VMEM(shape, BF16) for shape in shapes]


def reduce_semaphores(nz, nx, pieces):
    stages = nz.bit_length() - 1 + nx.bit_length() - 1 + 1
    shape = (pieces, stages, max(nx, nz // 2, 1))
    return [pltpu.SemaphoreType.DMA(shape)] * 3


class Total:
    def __init__(self, place, terms, landing, send, recv):
        self.place, self.terms, self.landing, self.send, self.recv = place, terms, landing, send, recv
        self.stages = len(place.partners())

    def copy(self, stage):
        device = self.place.partners()[stage]
        return remote(self.terms.at[stage], self.landing.at[stage], self.send.at[stage], self.recv.at[stage], device)

    def begin(self, stage):
        self.copy(stage).start()

    def finish(self, stage):
        self.copy(stage).wait()
        self.terms[stage + 1] = self.terms[stage] + self.landing[stage]


class ExpertGather:
    def __init__(self, place, in_own, out_own, in_full, out_full, send, recv, pair_send, pair_recv, here):
        self.place, z, xy, core = place, place.z, place.xy, place.core
        self.near = [
            pltpu.make_async_copy(in_own.at[core], in_full.at[z, xy, core], here.at[0]),
            pltpu.make_async_copy(out_own.at[core], out_full.at[z, xy, core], here.at[1]),
        ]
        self.pair = [
            remote(in_own.at[1 - core], in_full.at[z, xy, core], pair_send.at[0], pair_recv.at[0], place.sibling()),
            remote(out_own.at[1 - core], out_full.at[z, xy, core], pair_send.at[1], pair_recv.at[1], place.sibling()),
        ]
        self.gather = Gather(
            place, expert_pieces(in_full, out_full, lambda ref, columns: lambda zs, xs: [ref.at[zs, xs, :, :, columns]]),
            send, recv,
        )
        self.ticks = self.gather.ticks

    def begin(self):
        for copy in self.near:
            copy.start()

    def tick(self, now):
        if now == 0:
            for copy in self.pair:
                copy.start()
            for copy in self.near + self.pair:
                copy.wait()
        self.gather.tick(now)


EXPERT_CUTS = 4


def expert_pieces(in_ref, out_ref, make):
    pieces = []
    for ref in (in_ref, out_ref):
        cut = ref.shape[-1] // EXPERT_CUTS
        pieces += [make(ref, pl.ds(i * cut, cut)) for i in range(EXPERT_CUTS)]
    return pieces


def expert_gather_scratch(nz, nx):
    return [
        *gather_semaphores(nz, nx, 2 * EXPERT_CUTS, 1, False),
        pltpu.SemaphoreType.DMA((2,)),
        pltpu.SemaphoreType.DMA((2,)),
        pltpu.SemaphoreType.DMA((2,)),
    ]


def full_shapes(nz, nx, in_own, out_own):
    return [jax.ShapeDtypeStruct((nz, nx, 2) + own.shape[1:], BF16) for own in (in_own, out_own)]


class ExpertReduce:
    def __init__(self, place, in_terms, out_terms, in_sum, out_sum, buffers, send, recv, here):
        sources = expert_pieces(
            in_terms, out_terms, lambda ref, columns: lambda zs, xs, core: ref.at[zs, xs, :, :, columns]
        )
        targets = expert_pieces(in_sum, out_sum, lambda ref, columns: ref.at[:, :, columns])
        size = len(buffers) // len(sources)
        pieces = [
            (source, buffers[i * size : (i + 1) * size], target)
            for i, (source, target) in enumerate(zip(sources, targets))
        ]
        self.reduce = Reduce(place, pieces, False, send, recv, here)
        self.ticks, self.tick = self.reduce.ticks, self.reduce.tick


def expert_reduce_scratch(nz, nx, in_terms, out_terms):
    buffers = []
    for terms in (in_terms, out_terms):
        tail = terms.shape[2:4] + (terms.shape[4] // EXPERT_CUTS,)
        for _ in range(EXPERT_CUTS):
            buffers += reduce_buffers(nz, nx, tail, False)
    return buffers, list(reduce_semaphores(nz, nx, 2 * EXPERT_CUTS))


def sum_shapes(in_terms, out_terms):
    return [jax.ShapeDtypeStruct((2,) + terms.shape[3:], BF16) for terms in (in_terms, out_terms)]


def attend_pair(qkv, head, attended, log_total):
    n, d = attended.shape
    low = lax.broadcasted_iota(jnp.int32, (n, 128), 1) < HEAD
    one, zero = jnp.ones((), BF16), jnp.zeros((), BF16)
    query = qkv[:, pl.ds(pl.multiple_of(head * 128, 128), 128)]
    key = qkv[:, pl.ds(pl.multiple_of(d + head * 128, 128), 128)]
    value = qkv[:, pl.ds(pl.multiple_of(2 * d + head * 128, 128), 128)]
    values = [jnp.where(low, value, one), jnp.where(low, one, value)]
    queries = [jnp.where(low, query, zero), jnp.where(low, zero, query)]
    low = low[:BLOCK]
    allowed = lax.broadcasted_iota(jnp.int32, (BLOCK, BLOCK), 1) <= lax.broadcasted_iota(
        jnp.int32, (BLOCK, BLOCK), 0
    )
    for i in range(n // BLOCK):
        first, end = i * BLOCK, (i + 1) * BLOCK
        found = []
        for j in range(2):
            near = jnp.where(allowed, dot_last(queries[j][first:end], key[first:end]), MASKED)
            top = jnp.max(near, axis=-1, keepdims=True)
            if i:
                far = dot_last(queries[j][first:end], key[:first])
                top = jnp.maximum(top, jnp.max(far, axis=-1, keepdims=True))
            top = top * SCALE_LOG2
            out = dot(jnp.exp2(near * SCALE_LOG2 - top).astype(BF16), values[j][first:end])
            if i:
                out = out + dot(jnp.exp2(far * SCALE_LOG2 - top).astype(BF16), values[j][:first])
            found.append((out, top))
        (out_a, top_a), (out_b, top_b) = found
        total = pltpu.roll(jnp.where(low, out_b, out_a), HEAD, axis=1)
        attended[first:end, pl.ds(pl.multiple_of(head * 128, 128), 128)] = (
            jnp.where(low, out_a, out_b) / total
        ).astype(BF16)
        logs = (jnp.where(low, top_a, top_b) + jnp.log2(total)).T
        log_total[head, 0:1, first:end] = logs[0:1]
        log_total[head, 1:2, first:end] = logs[HEAD : HEAD + 1]


def attention_forward(nz, nx, tokens, qkv_full, out_full, vectors, slots, in_own, out_own):
    n, d = tokens.shape
    heads = d // 128

    def kernel(
        tokens_ref, w_ref, wo_ref, vec_ref, slots_ref, in_own, out_own,
        normed_hbm, qkv_hbm, attended_hbm, log_hbm, residual_hbm, rows_hbm, in_full, out_full,
        normed, qkv, attended, logs, residual, normed_two, picked, here, pair_send, pair_recv, *gather_scratch,
    ):
        place = Place(nz, nx)
        gather = ExpertGather(place, in_own, out_own, in_full, out_full, *gather_scratch)
        gather.begin()
        place.barrier()
        gather.tick(0)

        @pl.loop(0, n // BLOCK)
        def _(i):
            rows = pl.ds(pl.multiple_of(i * BLOCK, BLOCK), BLOCK)
            scaled, _ = row_stats(tokens_ref[rows].astype(F32))
            normed[rows] = (scaled * vec_ref[0:1, :d] + vec_ref[1:2, :d]).astype(BF16)
            qkv[rows] = (dot(normed[rows], w_ref[...]) + vec_ref[2:3, :]).astype(BF16)
            for k in range(n // BLOCK):
                if k % 2 == 1:
                    @pl.when(i == k)
                    def _(k=k):
                        gather.tick(1 + k // 2)

        saves = [
            pltpu.make_async_copy(normed, normed_hbm, here.at[0]),
            pltpu.make_async_copy(qkv, qkv_hbm, here.at[1]),
        ]
        for save in saves:
            save.start()

        @pl.loop(0, heads)
        def _(head):
            attend_pair(qkv, head, attended, logs)
            for k in range(heads):
                if 3 + k < gather.ticks - 2:
                    @pl.when(head == k)
                    def _(k=k):
                        gather.tick(3 + k)

        saves += [
            pltpu.make_async_copy(attended, attended_hbm, here.at[2]),
            pltpu.make_async_copy(logs, log_hbm, here.at[3]),
        ]
        for save in saves[2:]:
            save.start()
        for now in range(3 + heads, gather.ticks - 2):
            gather.tick(now)

        @pl.loop(0, n // BLOCK)
        def _(i):
            rows = pl.ds(pl.multiple_of(i * BLOCK, BLOCK), BLOCK)
            added = dot(attended[rows], wo_ref[...]) + vec_ref[0:1, 2 * d :]
            residual[rows] = tokens_ref[rows].astype(F32) + added
            scaled, _ = row_stats(residual[rows])
            normed_two[rows] = (scaled * vec_ref[0:1, d : 2 * d] + vec_ref[1:2, d : 2 * d]).astype(BF16)

        saves.append(pltpu.make_async_copy(residual, residual_hbm, here.at[4]))
        saves[-1].start()
        gather.tick(gather.ticks - 2)
        pick_rows(picked.at[1], slots_ref, normed_two[...], 1)
        theirs = remote(picked.at[1], rows_hbm.at[1], pair_send, pair_recv, place.sibling())
        theirs.start()
        pick_rows(picked.at[0], slots_ref, normed_two[...], 0)
        saves.append(pltpu.make_async_copy(picked.at[0], rows_hbm.at[0], here.at[5]))
        saves[-1].start()
        gather.tick(gather.ticks - 1)
        for save in saves:
            save.wait()
        theirs.wait()

    shapes = [
        jax.ShapeDtypeStruct((n, d), BF16),
        jax.ShapeDtypeStruct((n, 3 * d), BF16),
        jax.ShapeDtypeStruct((n, d), BF16),
        jax.ShapeDtypeStruct((heads, 8, n), F32),
        jax.ShapeDtypeStruct((n, d), F32),
        jax.ShapeDtypeStruct((2, MOST, d), BF16),
    ]
    return pl.pallas_call(
        kernel,
        out_shape=shapes + full_shapes(nz, nx, in_own, out_own),
        in_specs=[VMEM] * 5 + [HBM] * 2,
        out_specs=[HBM] * 8,
        scratch_shapes=[
            *[pltpu.VMEM(shape.shape, shape.dtype) for shape in shapes[:5]],
            pltpu.VMEM((n, d), BF16),
            pltpu.VMEM((2, MOST, d), BF16),
            pltpu.SemaphoreType.DMA((6,)),
            pltpu.SemaphoreType.DMA,
            pltpu.SemaphoreType.DMA,
            *expert_gather_scratch(nz, nx),
        ],
        compiler_params=remote_params(2, 60),
        name="attention_forward",
    )(tokens, qkv_full, out_full, vectors, slots, in_own, out_own)


def gelu_and_slope(values):
    root = math.sqrt(2 / math.pi)
    cube = 0.044715
    square = values * values
    bent = jnp.tanh(values * (root + root * cube * square))
    half = 0.5 * (1 + bent)
    slope = half + 0.5 * values * (1 - bent * bent) * (root + 3 * root * cube * square)
    return values * half, slope


TILE = 512


def expert_step(refs, side, steps):
    (rows_ref, grads_ref, in_ref, out_ref, bias_ref, in_grad, out_grad, bias_grad, turned, made, back) = refs
    step = pl.program_id(0)

    def beside(spot):
        for k in range(steps):
            @pl.when(step == k)
            def _(k=k):
                side(k, spot)

    @pl.when(step == 0)
    def _():
        turned[...] = rows_ref[...].T

    beside(0)
    hidden_pre = dot(rows_ref[...], in_ref[...]) + bias_ref[0:1, :]
    hidden, slope = gelu_and_slope(hidden_pre)
    hidden = hidden.astype(BF16)
    grad_pre = dot_last(grads_ref[...], out_ref[...]) * slope
    bias_grad[0:1, :] = jnp.sum(grad_pre, axis=0, keepdims=True)
    grad_pre = grad_pre.astype(BF16)
    beside(1)
    made[...] += dot(hidden, out_ref[...])
    back[...] += dot_last(grad_pre, in_ref[...])
    beside(2)
    out_grad[...] = dot(hidden.T, grads_ref[...]).astype(BF16)
    in_grad[...] = dot(turned[...], grad_pre).astype(BF16)
    beside(3)


def expert_specs(rows, d, width):
    whole = pl.BlockSpec((rows, d), lambda step: (0, 0), pipeline_mode=pl.Buffered(1))
    inputs = [
        whole,
        whole,
        pl.BlockSpec((d, TILE), lambda step: (0, step)),
        pl.BlockSpec((TILE, d), lambda step: (step, 0)),
        pl.BlockSpec((1, TILE), lambda step: (0, step)),
    ]
    outputs = [inputs[2], inputs[3], inputs[4]]
    shapes = [
        jax.ShapeDtypeStruct((d, width), BF16),
        jax.ShapeDtypeStruct((width, d), BF16),
        jax.ShapeDtypeStruct((1, width), F32),
    ]
    return inputs, outputs, shapes


def experts_first(nz, nx, rows, grads, in_full, out_full, bias, in_own, out_own):
    count, d = rows.shape
    width = in_full.shape[1]
    steps = width // TILE

    def kernel(
        rows_ref, grads_ref, in_ref, out_ref, bias_ref, in_own, out_own,
        in_grad, out_grad, bias_grad, out_bias_grad, made_hbm, back_hbm, in_next, out_next,
        turned, made, back, here, *gather_scratch,
    ):
        step = pl.program_id(0)
        place = Place(nz, nx)
        gather = ExpertGather(place, in_own, out_own, in_next, out_next, *gather_scratch)

        @pl.when(step == 0)
        def _():
            gather.begin()
            place.barrier()
            made[...] = jnp.zeros_like(made)
            back[...] = jnp.zeros_like(back)
            out_bias_grad[...] = jnp.broadcast_to(
                jnp.sum(grads_ref[...].astype(F32), axis=0, keepdims=True), out_bias_grad.shape
            )

        def side(k, spot):
            now = k * 4 + spot
            if now < gather.ticks:
                gather.tick(now)

        expert_step(
            (rows_ref, grads_ref, in_ref, out_ref, bias_ref, in_grad, out_grad, bias_grad, turned, made, back),
            side, steps,
        )

        @pl.when(step == steps - 1)
        def _():
            saves = [
                pltpu.make_async_copy(made, made_hbm, here.at[0]),
                pltpu.make_async_copy(back, back_hbm, here.at[1]),
            ]
            for save in saves:
                save.start()
            for now in range(steps * 4, gather.ticks):
                gather.tick(now)
            for save in saves:
                save.wait()

    inputs, outputs, shapes = expert_specs(count, d, width)
    total = jax.ShapeDtypeStruct((count, d), F32)
    return pl.pallas_call(
        kernel,
        grid=(steps,),
        out_shape=shapes + [jax.ShapeDtypeStruct((8, d), F32), total, total] + full_shapes(nz, nx, in_own, out_own),
        in_specs=inputs + [HBM] * 2,
        out_specs=outputs + [pl.BlockSpec((8, d), lambda step: (0, 0))] + [HBM] * 4,
        scratch_shapes=[
            pltpu.VMEM((d, count), BF16),
            pltpu.VMEM((count, d), F32),
            pltpu.VMEM((count, d), F32),
            pltpu.SemaphoreType.DMA((2,)),
            *expert_gather_scratch(nz, nx),
        ],
        compiler_params=remote_params(3, 62),
        name="experts_first",
    )(rows, grads, in_full, out_full, bias, in_own, out_own)


def experts_second(nz, nx, rows, grads, in_full, out_full, bias, out_bias, made_first, back_first, in_terms, out_terms):
    count, d = rows.shape
    width = in_full.shape[1]
    steps = width // TILE
    buffers, semaphores = expert_reduce_scratch(nz, nx, in_terms, out_terms)

    def kernel(
        rows_ref, grads_ref, in_ref, out_ref, bias_ref, out_bias_ref, made_hbm, back_hbm, in_terms, out_terms,
        in_grad, out_grad, bias_grad, made_rows, back_rows, in_sum, out_sum,
        turned, made, back, result, here, pair_send, pair_recv, *scratch,
    ):
        step = pl.program_id(0)
        place = Place(nz, nx)
        reduce = ExpertReduce(place, in_terms, out_terms, in_sum, out_sum, scratch[:-3], *scratch[-3:])
        half = count // 2

        @pl.when(step == 0)
        def _():
            loads = [
                pltpu.make_async_copy(made_hbm, made, here.at[0]),
                pltpu.make_async_copy(back_hbm, back, here.at[1]),
            ]
            for load in loads:
                load.start()
            place.barrier()
            reduce.tick(0)
            for load in loads:
                load.wait()

        def side(k, spot):
            now = k * 4 + spot
            if 0 < now < reduce.ticks:
                reduce.tick(now)

        expert_step(
            (rows_ref, grads_ref, in_ref, out_ref, bias_ref, in_grad, out_grad, bias_grad, turned, made, back),
            side, steps,
        )

        @pl.when(step == steps - 1)
        def _():
            result[0] = (made[...] + out_bias_ref[0:1, :]).astype(BF16)
            result[1] = back[...].astype(BF16)
            copies = []
            for i, target in enumerate((made_rows, back_rows)):
                copies.append(
                    remote(
                        result.at[i, pl.ds(half, half)], target.at[1], pair_send.at[i], pair_recv.at[i], place.sibling()
                    )
                )
                copies.append(pltpu.make_async_copy(result.at[i, pl.ds(0, half)], target.at[0], here.at[i]))
            for copy in copies:
                copy.start()
            for now in range(steps * 4, reduce.ticks):
                reduce.tick(now)
            for copy in copies:
                copy.wait()

    inputs, outputs, shapes = expert_specs(count, d, width)
    pair = jax.ShapeDtypeStruct((2, count // 2, d), BF16)
    return pl.pallas_call(
        kernel,
        grid=(steps,),
        out_shape=shapes + [pair, pair] + sum_shapes(in_terms, out_terms),
        in_specs=inputs + [pl.BlockSpec((1, d), lambda step: (0, 0))] + [HBM] * 4,
        out_specs=outputs + [HBM] * 4,
        scratch_shapes=[
            pltpu.VMEM((d, count), BF16),
            pltpu.VMEM((count, d), F32),
            pltpu.VMEM((count, d), F32),
            pltpu.VMEM((2, count, d), BF16),
            pltpu.SemaphoreType.DMA((2,)),
            pltpu.SemaphoreType.DMA((2,)),
            pltpu.SemaphoreType.DMA((2,)),
            *buffers,
            *semaphores,
        ],
        compiler_params=remote_params(4, 63),
        name="experts_second",
    )(rows, grads, in_full, out_full, bias, out_bias, made_first, back_first, in_terms, out_terms)


def norm_backward(values, gain, grad):
    scaled, inverse = row_stats(values)
    grad_scaled = grad * gain
    mean = jnp.mean(grad_scaled, axis=-1, keepdims=True)
    along = jnp.mean(grad_scaled * scaled, axis=-1, keepdims=True)
    term = inverse * (grad_scaled - mean - scaled * along)
    return term, jnp.sum(grad * scaled, axis=0, keepdims=True), jnp.sum(grad, axis=0, keepdims=True)


def attend_pair_backward(qkv, head, attended, grad, log_total, projected, turned):
    n, d = attended.shape
    low = lax.broadcasted_iota(jnp.int32, (n, 128), 1) < HEAD
    zero = jnp.zeros((), BF16)

    def columns(part):
        return pl.ds(pl.multiple_of(part * d + head * 128, 128), 128)

    query, key, value = (qkv[:, columns(part)] for part in range(3))
    grad = grad[:, columns(0)]
    product = (attended[:, columns(0)].astype(F32) * grad.astype(F32)).T
    inner = [jnp.sum(product[j * HEAD : (j + 1) * HEAD], axis=0, keepdims=True) for j in range(2)]
    logs = [log_total[head, j : j + 1, :] for j in range(2)]
    key_turned = key.T
    keys = [jnp.where(low, key, zero), jnp.where(low, zero, key)]
    values = [jnp.where(low, value, zero), jnp.where(low, zero, value)]
    low = low[:BLOCK]
    allowed = lax.broadcasted_iota(jnp.int32, (BLOCK, BLOCK), 0) <= lax.broadcasted_iota(
        jnp.int32, (BLOCK, BLOCK), 1
    )
    for i in range(n // BLOCK):
        first, end = i * BLOCK, (i + 1) * BLOCK
        found = []
        for j in range(2):
            grad_key = grad_value = 0.0
            for start, stop in ((first, end), (end, n)):
                if start == stop:
                    continue
                scores = dot_last(keys[j][first:end], query[start:stop])
                weights = jnp.exp2(scores * SCALE_LOG2 - logs[j][:, start:stop])
                if start == first:
                    weights = jnp.where(allowed, weights, 0.0)
                grad_weights = dot_last(values[j][first:end], grad[start:stop])
                grad_scores = (weights * (grad_weights - inner[j][:, start:stop])).astype(BF16)
                grad_value = grad_value + dot(weights.astype(BF16), grad[start:stop])
                grad_key = grad_key + dot(grad_scores, query[start:stop])
                part = dot(key_turned[j * HEAD : (j + 1) * HEAD, first:end], grad_scores)
                if i == 0:
                    turned[j * HEAD : (j + 1) * HEAD, start:stop] = part
                else:
                    turned[j * HEAD : (j + 1) * HEAD, start:stop] += part
            found.append((grad_key, grad_value))
        (key_a, value_a), (key_b, value_b) = found
        projected[first:end, columns(1)] = (jnp.where(low, key_a, key_b) * SCORE_SCALE).astype(BF16)
        projected[first:end, columns(2)] = jnp.where(low, value_a, value_b).astype(BF16)
    projected[:, columns(0)] = (turned[...].T * SCORE_SCALE).astype(BF16)


def attention_backward(
    nz, nx, residual, made_rows, back_rows, slots_turned, cotangent, out_full, vectors, attended, qkv, log_total, normed,
    in_terms, out_terms,
):
    n, d = cotangent.shape
    heads = d // 128
    count = made_rows.shape[0]
    buffers, semaphores = expert_reduce_scratch(nz, nx, in_terms, out_terms)

    def kernel(
        residual_hbm, made_ref, back_ref, slots_ref, cot_ref, wo_ref, vec_ref, att_ref, qkv_ref, logs_ref, normed_ref,
        in_terms, out_terms,
        block_hbm, grad_hbm, projected_hbm, qkv_terms, out_w_terms, sums, in_sum, out_sum,
        block, grad_res, branch, grad_att, turned, projected, wide, here, *scratch,
    ):
        place = Place(nz, nx)
        reduce = ExpertReduce(place, in_terms, out_terms, in_sum, out_sum, scratch[:-3], *scratch[-3:])
        load = pltpu.make_async_copy(residual_hbm, grad_res, here.at[0])
        load.start()
        place.barrier()
        reduce.tick(0)
        sums[...] = jnp.zeros_like(sums)
        load.wait()

        @pl.loop(0, n // BLOCK)
        def _(i):
            rows = pl.ds(pl.multiple_of(i * BLOCK, BLOCK), BLOCK)
            columns = lax.broadcasted_iota(jnp.int32, (BLOCK, MOST), 1)
            chosen = jnp.concatenate(
                [jnp.where(columns == slots_ref[rows, k : k + 1], 1.0, 0.0).astype(BF16) for k in range(2)], axis=1
            )
            values = grad_res[rows]
            block[rows] = (values + dot(chosen, made_ref[...])).astype(BF16)
            grad = dot(chosen, back_ref[...])
            term, gain_sum, shift_sum = norm_backward(values, vec_ref[0:1, d : 2 * d], grad)
            sums[1:2, :] += gain_sum
            sums[3:4, :] += shift_sum
            total = cot_ref[rows].astype(F32) + term
            grad_res[rows] = total
            low = total.astype(BF16)
            branch[rows] = low
            sums[6:7, :] += jnp.sum(low.astype(F32), axis=0, keepdims=True)
            grad_att[rows] = dot_last(low, wo_ref[...]).astype(BF16)
            for k in range(n // BLOCK):
                if k % 2 == 1:
                    @pl.when(i == k)
                    def _(k=k):
                        reduce.tick(1 + k // 2)

        saves = [
            pltpu.make_async_copy(block, block_hbm, here.at[0]),
            pltpu.make_async_copy(grad_res, grad_hbm, here.at[1]),
        ]
        for save in saves:
            save.start()

        @pl.loop(0, heads)
        def _(head):
            attend_pair_backward(qkv_ref, head, att_ref, grad_att, logs_ref, projected, turned)
            for k in range(heads):
                if 3 + k < reduce.ticks:
                    @pl.when(head == k)
                    def _(k=k):
                        reduce.tick(3 + k)

        saves.append(pltpu.make_async_copy(projected, projected_hbm, here.at[2]))
        saves[-1].start()
        written = [pltpu.make_async_copy(wide.at[0], out_w_terms, here.at[3])]
        wide[0] = dot(att_ref[...].T, branch[...]).astype(BF16)
        written[0].start()
        if 3 + heads < reduce.ticks:
            reduce.tick(3 + heads)
        normed_turned = normed_ref[...].T
        for part in range(3):
            columns = slice(part * d, (part + 1) * d)
            spot = (part + 1) % 2
            if part > 0:
                written[part - 1].wait()
            wide[spot] = dot(normed_turned, projected[:, columns]).astype(BF16)
            written.append(
                pltpu.make_async_copy(wide.at[spot], qkv_terms.at[:, pl.ds(part * d, d)], here.at[4 + part])
            )
            written[-1].start()
            if part != 1:
                sums[4 + part // 2 : 5 + part // 2, :] = jnp.sum(
                    projected[:, columns].astype(F32), axis=0, keepdims=True
                )
            if 4 + heads + part < reduce.ticks:
                reduce.tick(4 + heads + part)
        saves += written[2:]
        for now in range(7 + heads, reduce.ticks):
            reduce.tick(now)
        for save in saves:
            save.wait()

    return pl.pallas_call(
        kernel,
        out_shape=[
            jax.ShapeDtypeStruct((n, d), BF16),
            jax.ShapeDtypeStruct((n, d), F32),
            jax.ShapeDtypeStruct((n, 3 * d), BF16),
            jax.ShapeDtypeStruct((d, 3 * d), BF16),
            jax.ShapeDtypeStruct((d, d), BF16),
            jax.ShapeDtypeStruct((8, d), F32),
            *sum_shapes(in_terms, out_terms),
        ],
        in_specs=[HBM] + [VMEM] * 10 + [HBM] * 2,
        out_specs=[HBM] * 5 + [VMEM] + [HBM] * 2,
        scratch_shapes=[
            pltpu.VMEM((n, d), BF16),
            pltpu.VMEM((n, d), F32),
            pltpu.VMEM((n, d), BF16),
            pltpu.VMEM((n, d), BF16),
            pltpu.VMEM((128, n), F32),
            pltpu.VMEM((n, 3 * d), BF16),
            pltpu.VMEM((2, d, d), BF16),
            pltpu.SemaphoreType.DMA((7,)),
            *buffers,
            *semaphores,
        ],
        compiler_params=remote_params(5, 63),
        name="attention_backward",
    )(
        residual, made_rows, back_rows, slots_turned, cotangent, out_full, vectors, attended, qkv, log_total, normed,
        in_terms, out_terms,
    )


def last_sums(nz, nx, projected, qkv_full, grad_res, tokens, vectors, small, qkv_terms, out_terms):
    n, d = tokens.shape
    depth = qkv_terms.shape[3]
    buffers = []
    for _ in range(4):
        buffers += reduce_buffers(nz, nx, (depth, d), True)
    size = len(buffers) // 4
    partners = nz.bit_length() - 1 + nx.bit_length() - 1 + 1

    def kernel(
        projected_ref, w_ref, grad_ref, tokens_ref, vec_ref, small_ref, qkv_terms, out_terms,
        input_grad, small_sum, qkv_sum, out_sum,
        terms, landing, small_send, small_recv, *scratch,
    ):
        place = Place(nz, nx)

        def piece(i):
            if i == 3:
                return lambda zs, xs, core: out_terms.at[zs, xs, core], scratch[3 * size : 4 * size], out_sum
            columns = pl.ds(i * d, d)
            return (
                lambda zs, xs, core: qkv_terms.at[zs, xs, core, :, columns],
                scratch[i * size : (i + 1) * size],
                qkv_sum.at[:, columns],
            )

        reduce = Reduce(place, [piece(i) for i in (3, 0, 1, 2)], True, *scratch[-3:])
        total = Total(place, terms, landing, small_send, small_recv)
        place.barrier()
        reduce.tick(0)
        terms[0] = small_ref[...]

        @pl.loop(0, n // BLOCK)
        def _(i):
            rows = pl.ds(pl.multiple_of(i * BLOCK, BLOCK), BLOCK)
            grad = dot_last(projected_ref[rows], w_ref[...])
            term, gain_sum, shift_sum = norm_backward(tokens_ref[rows].astype(F32), vec_ref[0:1, :d], grad)
            input_grad[rows] = grad_ref[rows] + term
            terms[0, 0:1, :] += gain_sum
            terms[0, 2:3, :] += shift_sum
            for k in range(n // BLOCK):
                @pl.when(i == k)
                def _(k=k):
                    reduce.tick(1 + k)

        stage = 0
        for now in range(1 + n // BLOCK, reduce.ticks):
            if stage < total.stages:
                total.begin(stage)
            reduce.tick(now)
            if stage < total.stages:
                total.finish(stage)
                stage += 1
        for late in range(stage, total.stages):
            total.begin(late)
            total.finish(late)
        small_sum[...] = terms[total.stages]

    shape = small.shape
    return pl.pallas_call(
        kernel,
        out_shape=[
            jax.ShapeDtypeStruct((n, d), F32),
            jax.ShapeDtypeStruct(shape, F32),
            jax.ShapeDtypeStruct((depth, 3 * d), BF16),
            jax.ShapeDtypeStruct((depth, d), BF16),
        ],
        in_specs=[VMEM] * 6 + [HBM] * 2,
        out_specs=[VMEM] * 2 + [HBM] * 2,
        scratch_shapes=[
            pltpu.VMEM((partners + 1,) + shape, F32),
            pltpu.VMEM((partners,) + shape, F32),
            pltpu.SemaphoreType.DMA((partners,)),
            pltpu.SemaphoreType.DMA((partners,)),
            *buffers,
            *reduce_semaphores(nz, nx, 4),
        ],
        compiler_params=remote_params(6, 60),
        name="last_sums",
    )(projected, qkv_full, grad_res, tokens, vectors, small, qkv_terms, out_terms)


def shards(
    nz, nx, tokens, norm_gain, norm_bias, w_qkv, attn_bias, w_attn_out, expert_in, expert_in_bias, expert_out,
    expert_out_bias, expert_ids, running_load, cotangent,
):
    n, d = tokens.shape
    devices = nz * nx * 2
    core = lax.axis_index("core")
    me = lax.axis_index(("dp", "xy", "core"))
    share = norm_gain.shape[1]
    in_depth, width = expert_in.shape[1:]
    out_depth = expert_out.shape[1]
    part = out_depth // CHUNKS

    ids = expert_ids[:, 0]
    second = (ids == 1).astype(jnp.int32)
    before = jnp.cumsum(second)
    count_second = before[-1]
    rank = jnp.where(ids == 1, before - 1, jnp.arange(n, dtype=jnp.int32) - before)
    own = ids == core
    slots = jnp.stack([jnp.where(own, rank, -1), jnp.where(own, -1, rank)])
    slots = jnp.concatenate([slots, jnp.full((6, n), -1, jnp.int32)])
    slots_turned = slots.T

    digits = jnp.stack([count_second // 32, count_second % 32]).astype(BF16)
    small = jnp.concatenate(
        [
            norm_gain.reshape(-1),
            norm_bias.reshape(-1),
            attn_bias.reshape(-1),
            expert_out_bias.reshape(-1),
            expert_in_bias.reshape(-1),
            digits,
        ]
    )
    used = 9 * share + 2 * out_depth
    small = jnp.concatenate([small, jnp.zeros((2048 - used - 2,), BF16)]).reshape(16, 128)

    qkv_full, out_full, small_full, grad_rows = attention_weights(
        nz, nx, w_qkv, w_attn_out, small, cotangent, slots
    )
    qkv_full = qkv_full.reshape(d, 3 * d)
    out_full = out_full.reshape(d, d)
    small_full = small_full.reshape(devices, 2048)
    rows = small_full[:, : 9 * share].reshape(devices, 9, share).transpose(1, 0, 2).reshape(9, d).astype(F32)
    none = jnp.zeros((d,), F32)
    vectors = jnp.concatenate(
        [
            jnp.stack(
                [
                    jnp.concatenate([rows[0], rows[1], rows[6]]),
                    jnp.concatenate([rows[2], rows[3], none]),
                    jnp.concatenate([rows[4], none, rows[5]]),
                ]
            ),
            jnp.zeros((5, 3 * d), F32),
        ]
    )
    out_bias = lax.dynamic_slice_in_dim(rows, 7 + core, 1)
    in_bias = small_full[:, 9 * share : used].reshape(devices, EXPERTS, CHUNKS, part)
    in_bias = lax.dynamic_index_in_dim(in_bias, core, 1, keepdims=False)
    in_bias = in_bias.transpose(1, 0, 2).reshape(CHUNKS, 1, devices * part).astype(F32)
    counts = small_full[:, used : used + 2].astype(jnp.int32)
    total_second = jnp.sum(counts[:, 0] * 32 + counts[:, 1])
    expert_counts = jnp.stack([n * devices - total_second, total_second])
    expert_load = 0.9 * running_load + 0.1 * (expert_counts.astype(F32) * EXPERTS / (n * devices))

    in_own = expert_in.reshape(EXPERTS, in_depth, devices, CHUNKS, part).transpose(3, 0, 1, 2, 4)
    in_own = in_own.reshape(CHUNKS, EXPERTS, in_depth, devices * part)
    out_own = expert_out.reshape(EXPERTS, CHUNKS, part, d)

    normed, qkv, attended, log_total, residual, picked, in_a, out_a = attention_forward(
        nz, nx, tokens, qkv_full, out_full, vectors, slots, in_own[0], out_own[:, 0]
    )
    picked = picked.reshape(2 * MOST, d)
    grad_rows = grad_rows.reshape(2 * MOST, d)
    wide = (d, devices * part)
    tall = (devices * part, d)
    in_grad_a, out_grad_a, bias_grad_a, out_bias_grad, made, back, in_b, out_b = experts_first(
        nz, nx, picked, grad_rows, in_a.reshape(wide), out_a.reshape(tall), in_bias[0], in_own[1], out_own[:, 1]
    )
    in_split = (nz, nx, 2, in_depth, devices * part)
    out_split = (nz, nx, 2, part, d)
    in_grad_b, out_grad_b, bias_grad_b, made_rows, back_rows, in_sum_a, out_sum_a = experts_second(
        nz, nx, picked, grad_rows, in_b.reshape(wide), out_b.reshape(tall), in_bias[1], out_bias, made, back,
        in_grad_a.reshape(in_split), out_grad_a.reshape(out_split),
    )
    block_out, grad_res, projected, qkv_terms, out_terms, sums, in_sum_b, out_sum_b = attention_backward(
        nz, nx, residual, made_rows.reshape(2 * MOST, d), back_rows.reshape(2 * MOST, d), slots_turned, cotangent,
        out_full, vectors, attended, qkv, log_total, normed,
        in_grad_b.reshape(in_split), out_grad_b.reshape(out_split),
    )
    bias_rows = jnp.concatenate([bias_grad_a, bias_grad_b], axis=1).reshape(-1, d)
    lines = bias_rows.shape[0]
    small_terms = jnp.concatenate([sums, jnp.zeros((2 + 2 * lines + (-(2 + 2 * lines)) % 8, d), F32)])
    small_terms = lax.dynamic_update_slice(small_terms, out_bias_grad[:1], (8 + core, 0))
    small_terms = lax.dynamic_update_slice(small_terms, bias_rows, (10 + lines * core, 0))
    input_grad, small_sum, qkv_sum, out_sum = last_sums(
        nz, nx, projected, qkv_full, grad_res, tokens, vectors, small_terms,
        qkv_terms.reshape(nz, nx, 2, d // devices, 3 * d), out_terms.reshape(nz, nx, 2, d // devices, d),
    )
    mine = lax.dynamic_slice_in_dim(small_sum[:10], me * share, share, axis=1)
    bias_sum = small_sum[10 : 10 + 2 * lines].reshape(EXPERTS, CHUNKS, devices * part)
    bias_sum = lax.dynamic_slice_in_dim(bias_sum, me * part, part, axis=2).reshape(EXPERTS, out_depth)
    in_sum = jnp.stack([in_sum_a, in_sum_b]).reshape(CHUNKS, EXPERTS, in_depth, devices, part)
    in_sum = in_sum.transpose(1, 2, 3, 0, 4).reshape(EXPERTS, in_depth, width).astype(F32)
    out_sum_experts = jnp.concatenate([out_sum_a, out_sum_b], axis=1).astype(F32)
    return (
        block_out,
        input_grad,
        mine[0:2],
        mine[2:4],
        qkv_sum.astype(F32),
        mine[4:7],
        out_sum.astype(F32),
        in_sum,
        bias_sum,
        out_sum_experts,
        mine[8:10],
        expert_counts,
        expert_load,
    )


def solution(mesh):
    nz, nx = mesh.shape["dp"], mesh.shape["fsdp"] // 2
    fine = Mesh(mesh.devices.reshape(nz, nx, 2), ("dp", "xy", "core"))
    every = ("dp", "xy", "core")
    row, column, middle = P(every, None), P(None, every), P(None, every, None)
    return jax.shard_map(
        functools.partial(shards, nz, nx),
        mesh=fine,
        in_specs=(
            row, column, column, row, column, row, middle, column, middle, column, row, P(), row,
        ),
        out_specs=(row, row, column, column, row, column, row, middle, column, middle, column, P(), P()),
        check_vma=False,
    )
```

time: 2250 us -> 676 us (0.30)
  waiting for transfers between devices: 1180 us -> 0 us
  Pallas kernels: 0 us -> 614 us
  matrix products: 421 us -> 0 us
  blocking collectives: 272 us -> 0 us
  other arithmetic: 213 us -> 10.5 us
  local copies, waits for them, and re-layouts: 118 us -> 38.6 us
    reduce_scatter x6 -> x0, waiting for transfers between devices: 1040 us -> none  [the longest x2 371 us: shards(): lax.psum_scatter(grad_terms[0], ('dp', 'fsdp'), scatter_dimension=0, tile...]
    pallas_call x0 -> x6, Pallas kernels: none -> 614 us  [the longest x1 125 us: experts_second(): pl.pallas_call(kernel, grid=(steps,), out_shape=shapes + [pair, pair] + s...]
    dot_general x32 -> x0, matrix products: 421 us -> none  [the longest x6 75.8 us: contract_rows(): lax.dot_general(left_side, right_side, (((0,), (0,)), ((), ())), preferre...]
    all_gather x5 -> x0, blocking collectives: 193 us -> none  [the longest x2 79.8 us: shards(): lax.all_gather(expert_in_bias[expert], ('dp', 'fsdp'), axis=0, tiled=True)]
    unnamed x18 -> x0, waiting for transfers between devices: 143 us -> none
    unnamed x2 -> x0, blocking collectives: 79.1 us -> none
    reduce_sum x17 -> x1, other arithmetic: 67.6 us -> 0.71 us  [shards(): total_second = jnp.sum(counts[:, 0] * 32 + counts[:, 1])]
    convert_element_type x13 -> x8, other arithmetic: 66.5 us -> 6.35 us  [the longest x1 2.04 us: shards(): jnp.concatenate([out_sum_a, out_sum_b], axis=1).astype(F32)]
  transfers between devices with their start and end apart: 15 -> 0, of which waited for: 8 -> 0; matrix products, arithmetic and copies ran while one was open for 19% -> 0% of each run, Pallas kernels for 0% -> 0%
where the time goes in v1:
time: 676 us; the launch traced here: 668 us
  Pallas kernels  614 us (91%)
  local copies, waits for them, and re-layouts  38.6 us (6%)
  other arithmetic  10.5 us (2%)
    pallas_call x1, Pallas kernels, experts_second(): pl.pallas_call(kernel, grid=(steps,), out_shape=shapes + [pair, pair] + s...  125 us
    pallas_call x1, Pallas kernels, experts_first(): pl.pallas_call(kernel, grid=(steps,), out_shape=shapes + [jax.ShapeDtypeS...  123 us
    pallas_call x1, Pallas kernels, attention_backward(): pl.pallas_call(kernel, out_shape=[jax.ShapeDtypeStruct((n, d), BF16), jax...  119 us
    pallas_call x1, Pallas kernels, attention_forward(): pl.pallas_call(kernel, out_shape=shapes + full_shapes(nz, nx, in_own, out...  114 us
    pallas_call x1, Pallas kernels, last_sums(): pl.pallas_call(kernel, out_shape=[jax.ShapeDtypeStruct((n, d), F32), jax....  72.1 us
    pallas_call x1, Pallas kernels, attention_weights(): pl.pallas_call(kernel, out_shape=[jax.ShapeDtypeStruct((nz, nx, 2, depth,...  61.5 us

profile of v1, /device:TPU:0, one launch (start us, length us, event | category | flops | bytes accessed | tf_op | source)
XLA Modules:
  0.0 668.2 jit_solution(8719347485662858823)
XLA Ops:
  9.8 1.6 copy-done.2
  11.4 0.9 copy-done.6
  13.2 61.5 %attention_weights.1 = (bf16[4,4,2,32,3072]{4,3,2,1,0:T(8,128)(2,1)S(1)}, bf16[4,4,2,32,1024]{4,3,2,1,0:T(8,128)(2,1)S(1)}, bf16[4,4,2,16,128]{4,3,2,1,0:T(8,128)(2,1)S(1)}, bf16[2,640,1024]{2,1,0:T(8,128)(2,1)S(1)}) custom-call(bf16[32,3072]{1,0:T(8,128)(2,1)S(1)} %copy-done.6, bf16[32,1024]{1,0:T(8,128)(2,1)S(1)} %copy-done.7, ...), custom_call_target="tpu_custom_call" | custom-call | tf_op jit(solution)/shard_map/attention_weights/pallas_call | solution.py:201
  74.7 2.6 copy-done
  77.4 1.5 copy-done.1
  78.9 1.3 copy-done.3
  82.3 1.1 reshape.272
  83.7 1.2 squeeze.55.in_own
  85.7 113.7 %attention_forward.1 = (bf16[1024,1024]{1,0:T(8,128)(2,1)}, bf16[1024,3072]{1,0:T(8,128)(2,1)}, bf16[1024,1024]{1,0:T(8,128)(2,1)}, f32[8,8,1024]{2,1,0:T(8,128)...) custom-call(bf16[1024,1024]{1,0:T(8,128)(2,1)} %tokens_ref.3, ...), custom_call_target="tpu_custom_call" | custom-call | tf_op jit(solution)/shard_map/attention_forward/pallas_call | solution.py:547
  200.3 1.2 squeeze.58.in_own
  201.5 122.7 %experts_first.1 = (bf16[1024,2048]{1,0:T(8,128)(2,1)}, bf16[2048,1024]{1,0:T(8,128)(2,1)}, f32[1,2048]{1,0:T(1,128)}, f32[8,1024]{1,0:T(8,128)}, f32[1280,1024]...) custom-call(bf16[1280,1024]{1,0:T(8,128)(2,1)} %bitcast.80, ...), custom_call_target="tpu_custom_call" | custom-call | tf_op jit(solution)/shard_map/experts_first/pallas_call | solution.py:676
  325.7 124.8 %experts_second.1 = (bf16[1024,2048]{1,0:T(8,128)(2,1)}, bf16[2048,1024]{1,0:T(8,128)(2,1)}, f32[1,2048]{1,0:T(1,128)}, bf16[2,640,1024]{2,1,0:T(8,128)(2,1)}, b...) custom-call(bf16[1280,1024]{1,0:T(8,128)(2,1)} %bitcast.81, ...), custom_call_target="tpu_custom_call" | custom-call | tf_op jit(solution)/shard_map/experts_second/pallas_call | solution.py:754
  450.6 1.0 copy.75
  451.6 119.5 %attention_backward.1 = (bf16[1024,1024]{1,0:T(8,128)(2,1)}, f32[1024,1024]{1,0:T(8,128)}, bf16[1024,3072]{1,0:T(8,128)(2,1)}, bf16[1024,3072]{1,0:T(8,128)(2,1)...) custom-call(f32[1024,1024]{1,0:T(8,128)} %get-tuple-element.55.resid, ...), custom_call_target="tpu_custom_call" | custom-call | tf_op jit(solution)/shard_map/attention_backward/pallas_call | solution.py:928
  571.1 2.0 maximum_convert_fusion
  573.1 1.5 stack.45
  575.4 1.9 copy.76
  577.4 3.2 reshape.293
  582.4 72.1 %last_sums.1 = (f32[1024,1024]{1,0:T(8,128)}, f32[24,1024]{1,0:T(8,128)}, bf16[32,3072]{1,0:T(8,128)(2,1)}, bf16[32,1024]{1,0:T(8,128)(2,1)}) custom-call(bf16[1024,3072]{1,0:T(8,128)(2,1)} %get-tuple-element.75.projected_ref, bf16[1024,3072]{1,0:T(8,128)(2,1)} %bitcast.73, f32[1024,1024]{1,0:T(8,128)} %get-tuple-element.76.grad_ref, ...), custom_call_target="tpu_custom_call" | custom-call | tf_op jit(solution)/shard_map/last_sums/pallas_call | solution.py:1020
  654.6 1.7 convert_element_type.71
  656.3 1.5 convert_element_type.72
  663.0 1.4 multiply_add_fusion
  664.4 1.3 copy.89
  665.7 2.0 copy.90
  (105 shorter events, 20.1 us)
Async XLA Ops:
  9.8 1.6 copy-start.2
  11.4 0.9 copy-start.6
  12.3 0.8 copy-start.7
  13.2 70.5 %copy-start.4 = (s32[8,1024]{1,0:T(8,128)}, s32[8,1024]{1,0:T(8,128)S(1)}, u32[]{:S(2)}) copy-start(s32[8,1024]{1,0:T(8,128)S(1)} %add_add_fusion.slots_ref) | copy-start | bytes 98308
  13.2 69.1 %copy-start.10 = (bf16[2,32,4096]{2,1,0:T(8,128)(2,1)S(1)}, bf16[2,32,4096]{2,1,0:T(8,128)(2,1)}, u32[]{:S(2)}) copy-start(bf16[2,32,4096]{2,1,0:T(8,128)(2,1)} %param.19) | copy-start | bytes 1572868
  74.7 2.7 copy-start
  77.4 1.5 copy-start.1
  78.9 1.3 copy-start.3
  80.2 4.7 copy-start.11
  325.7 124.8 %copy-start.5 = (s32[8,1024]{1,0:T(8,128)S(1)}, s32[8,1024]{1,0:T(8,128)}, u32[]{:S(2)}) copy-start(s32[8,1024]{1,0:T(8,128)} %copy-done.4) | copy-start | bytes 98308
  451.6 119.5 %copy-start.14 = (bf16[2,64,1024]{2,1,0:T(8,128)(2,1)S(1)}, bf16[2,64,1024]{2,1,0:T(8,128)(2,1)}, u32[]{:S(2)}) copy-start(bf16[2,64,1024]{2,1,0:T(8,128)(2,1)} %get-tuple-element.89) | copy-start | bytes 786436
  451.6 123.0 %copy-start.13 = (bf16[2,32,2048]{2,1,0:T(8,128)(2,1)S(1)}, bf16[2,32,2048]{2,1,0:T(8,128)(2,1)}, u32[]{:S(2)}) copy-start(bf16[2,32,2048]{2,1,0:T(8,128)(2,1)} %get-tuple-element.87) | copy-start | bytes 786436
  575.4 5.1 copy-start.16
  575.4 5.1 copy-start.17
  575.4 5.2 copy-start.15
  581.8 0.6 copy-start.12
  582.4 80.6 %copy-start.18 = (f32[2]{0:T(128)S(1)}, f32[2]{0:T(128)}, u32[]{:S(2)}) copy-start(f32[2]{0:T(128)} %param.24) | copy-start | bytes 28
  582.4 82.0 %copy-start.9 = (bf16[1024,1024]{1,0:T(8,128)(2,1)S(1)}, bf16[1024,1024]{1,0:T(8,128)(2,1)}, u32[]{:S(2)}) copy-start(bf16[1024,1024]{1,0:T(8,128)(2,1)} %get-tuple-element.126) | copy-start | bytes 6291460
  663.0 2.7 copy-start.8

commit v2 on v0

v2 whole, which is shorter than its diff:
```python
import functools
import math

import jax
import jax.numpy as jnp
from jax import lax
from jax.experimental import pallas as pl
from jax.experimental.pallas import tpu as pltpu
from jax.sharding import Mesh, PartitionSpec as P

BF16 = jnp.bfloat16
F32 = jnp.float32
MESH_ID = pl.DeviceIdType.MESH

HEAD = 64
MOST = 640
EXPERTS = 2
CHUNKS = 2
CUTS = 4
AHEAD = 1
NORM_EPS = 1e-05
SCORE_SCALE = 0.125
SCALE_LOG2 = SCORE_SCALE * math.log2(math.e)
MASKED = -1e30
BLOCK = 256
MIB = 1 << 20
ALL = slice(None)
HBM = pl.BlockSpec(memory_space=pl.ANY)
VMEM = pl.BlockSpec(memory_space=pltpu.VMEM)


def dot(left, right):
    return lax.dot_general(left, right, (((1,), (0,)), ((), ())), preferred_element_type=F32)


def dot_last(left, right):
    return lax.dot_general(left, right, (((1,), (1,)), ((), ())), preferred_element_type=F32)


def row_stats(values):
    center = values - jnp.mean(values, axis=-1, keepdims=True)
    spread = jnp.mean(center * center, axis=-1, keepdims=True)
    inverse = lax.rsqrt(spread + NORM_EPS)
    return center * inverse, inverse


def as_rows(values, rows):
    if values.dtype == BF16 and values.shape[-2] % 16:
        return values.astype(F32).reshape(rows, values.shape[-1]).astype(BF16)
    return values.reshape(rows, values.shape[-1])


def split_rows(values, shape):
    if values.dtype == BF16 and shape[-2] % 16:
        return values.astype(F32).reshape(shape).astype(BF16)
    return values.reshape(shape)


class Place:
    def __init__(self, nz, nx):
        self.nz, self.nx = nz, nx
        self.bits_z, self.bits_x = nz.bit_length() - 1, nx.bit_length() - 1
        self.z, self.xy, self.core = lax.axis_index("dp"), lax.axis_index("xy"), lax.axis_index("core")
        self.flip_z = [(1 - 2 * lax.rem(lax.div(self.z, 2**k), 2)) * 2**k for k in range(self.bits_z)]
        self.flip_x = [(1 - 2 * lax.rem(lax.div(self.xy, 2**k), 2)) * 2**k for k in range(self.bits_x)]

    def step_x(self, k, core=None):
        core = self.core if core is None else core
        return (1 - core) * self.flip_x[k] + core * self.flip_x[self.bits_x - 1 - k]

    def span_x(self, which, core=None):
        return self.xy + sum(self.step_x(k, core) for k in range(self.bits_x) if which >> k & 1)

    def span_z(self, which):
        return self.z + sum(self.flip_z[k] for k in range(self.bits_z) if which >> k & 1)

    def partners(self):
        found = [(self.z + flip, self.xy, self.core) for flip in self.flip_z]
        found += [(self.z, self.xy + flip, self.core) for flip in self.flip_x]
        return found + [self.sibling()]

    def sibling(self):
        return (self.z, self.xy, 1 - self.core)

    def barrier(self):
        semaphore = pltpu.get_barrier_semaphore()
        partners = self.partners()
        for partner in partners:
            pl.semaphore_signal(semaphore, inc=1, device_id=partner, device_id_type=MESH_ID)
        pl.semaphore_wait(semaphore, len(partners))


class Copies:
    def __init__(self, send, recv, near):
        self.send, self.recv, self.near = send, recv, near
        self.far_names, self.near_names = {}, {}

    def far(self, name, src, dst, device):
        i = self.far_names.setdefault(name, len(self.far_names))
        return pltpu.make_async_remote_copy(
            src_ref=src, dst_ref=dst, send_sem=self.send.at[i], recv_sem=self.recv.at[i],
            device_id=device, device_id_type=MESH_ID,
        )

    def local(self, name, src, dst, slot=None):
        if slot is not None:
            self.near_names.setdefault((name, 0), len(self.near_names))
            self.near_names.setdefault((name, 1), len(self.near_names))
            return pltpu.make_async_copy(src, dst, self.near.at[self.near_names[name, 0] + slot])
        i = self.near_names.setdefault(name, len(self.near_names))
        return pltpu.make_async_copy(src, dst, self.near.at[i])


def semaphores(far, near):
    return [
        pltpu.SemaphoreType.DMA((far,)),
        pltpu.SemaphoreType.DMA((far,)),
        pltpu.SemaphoreType.DMA((near,)),
    ]


class Stream:
    def __init__(self, pieces):
        self.pieces = pieces

    def tick(self, now):
        for stage in range(max(self.stages(p) for p in self.pieces) - 1, 0, -1):
            piece = now - stage
            if 0 <= piece < len(self.pieces) and stage < self.stages(self.pieces[piece]):
                self.finish(piece, stage - 1)
                self.begin(piece, stage)
        for piece in range(0 if now == 0 else now + AHEAD, now + AHEAD + 1):
            if piece < len(self.pieces):
                self.begin(piece, 0)

    def need(self, piece):
        self.finish(piece, self.stages(self.pieces[piece]) - 1)


class Gather(Stream):
    def __init__(self, name, place, copies, pieces):
        super().__init__(pieces)
        self.name, self.place, self.made = name, place, copies

    def stages(self, piece):
        return self.place.bits_z + self.place.bits_x + (piece[1] is not None)

    def copies(self, piece, stage):
        place = self.place
        region, to_sibling = self.pieces[piece]
        found = []
        if stage < place.bits_z:
            bit = place.bits_z - 1 - stage
            device = (place.z + place.flip_z[bit], place.xy, place.core)
            for held in range(2**stage):
                found += [(ref, device) for ref in region(place.span_z(held << (bit + 1)), place.xy)]
        elif stage < place.bits_z + place.bits_x:
            step = stage - place.bits_z
            device = (place.z, place.xy + place.step_x(step), place.core)
            for held in range(2**step):
                found += [(ref, device) for ref in region(ALL, place.span_x(held))]
        else:
            found += [(ref, place.sibling()) for ref in to_sibling]
        return [
            self.made.far((self.name, piece, stage, i), ref, ref, device) for i, (ref, device) in enumerate(found)
        ]

    def begin(self, piece, stage):
        for copy in self.copies(piece, stage):
            copy.start()

    def finish(self, piece, stage):
        for copy in self.copies(piece, stage):
            copy.wait()


class Reduce(Stream):
    def __init__(self, name, place, copies, pieces):
        super().__init__(pieces)
        self.name, self.place, self.made = name, place, copies

    def stages(self, piece):
        return self.place.bits_z + self.place.bits_x + 1

    def plan(self, piece, stage):
        place = self.place
        source, landing, spare, target, owner = self.pieces[piece]
        acc = landing[0]
        nx, bits_x = place.nx, place.bits_x
        far, near, sums = [], [], []
        slot = stage
        if owner == "first":
            if stage == 0:
                for r in range(nx):
                    there = 1 - place.core
                    far.append((source(ALL, place.span_x(r, there), there), acc.at[r], place.sibling()))
                    near.append((source(ALL, place.span_x(r), place.core), spare.at[r]))
                    sums.append((acc.at[r], spare.at[r]))
                return far, near, sums
            stage -= 1
        if stage < bits_x:
            k = bits_x - 1 - stage
            device = (place.z, place.xy + place.step_x(k), place.core)
            if slot == 0:
                for j in range(2**k):
                    far.append((source(ALL, place.span_x(2**k + j), place.core), acc.at[j], device))
                    near.append((source(ALL, place.span_x(j), place.core), spare.at[j]))
                    sums.append((acc.at[j], spare.at[j]))
            else:
                far.append((acc.at[pl.ds(2**k, 2**k)], landing[slot], device))
                sums += [(acc.at[j], landing[slot].at[j]) for j in range(2**k)]
        else:
            bit = stage - bits_x
            device = (place.z + place.flip_z[bit], place.xy, place.core)
            for s in range(2 ** (place.bits_z - 1 - bit)):
                upper = s << (bit + 1)
                far.append((acc.at[0, place.span_z(upper + 2**bit)], landing[slot].at[s], device))
                sums.append((acc.at[0, place.span_z(upper)], landing[slot].at[s]))
        return far, near, sums

    def made_copies(self, piece, stage, far, near):
        made = [
            self.made.far((self.name, piece, stage, i), src, dst, device) for i, (src, dst, device) in enumerate(far)
        ]
        return made + [self.made.local((self.name, piece, stage, i), src, dst) for i, (src, dst) in enumerate(near)]

    def last(self, piece, begin):
        place, core = self.place, self.place.core
        _, landing, _, target, owner = self.pieces[piece]
        mine = landing[0].at[0, place.z]
        name = (self.name, piece, "last")
        if owner == "both":
            there = self.made.far(name, mine.at[1 - core], target(core), place.sibling())
            here = self.made.local(name, mine.at[core], target(core))
            for copy in (there, here):
                copy.start() if begin else copy.wait()
            return
        there = self.made.far(name, mine, target(core), place.sibling())
        here = self.made.local(name, mine, target(core))

        @pl.when(core == owner)
        def _():
            if begin:
                here.start()
            else:
                here.wait()
                there.wait_recv()

        @pl.when(core != owner)
        def _():
            there.start() if begin else there.wait_send()

    def begin(self, piece, stage):
        if stage == self.stages(self.pieces[piece]) - 1 and self.pieces[piece][4] != "first":
            self.last(piece, True)
            return
        far, near, _ = self.plan(piece, stage)
        for copy in self.made_copies(piece, stage, far, near):
            copy.start()

    def finish(self, piece, stage):
        owner = self.pieces[piece][4]
        final = stage == self.stages(self.pieces[piece]) - 1
        if final and owner != "first":
            self.last(piece, False)
            return
        far, near, sums = self.plan(piece, stage)
        for copy in self.made_copies(piece, stage, far, near):
            copy.wait()
        for total, landed in sums:
            if len(total.shape) > 3 or (owner == "first" and len(total.shape) > 2):
                @pl.loop(0, total.shape[0])
                def _(i, total=total, landed=landed):
                    total[i] = (total[i].astype(F32) + landed[i].astype(F32)).astype(BF16)
            else:
                total[...] = (total[...].astype(F32) + landed[...].astype(F32)).astype(BF16)
        if final:
            here = self.made.local((self.name, piece, "last"), self.pieces[piece][1][0].at[0, self.place.z], self.pieces[piece][3])
            here.start()
            here.wait()


def landing_shapes(nz, nx, tail, first):
    bits_z, bits_x = nz.bit_length() - 1, nx.bit_length() - 1
    shapes = [(nx, nz) + tail] if first else []
    shapes += [(2**k, nz) + tail for k in reversed(range(bits_x))]
    return shapes + [(2 ** (bits_z - 1 - bit),) + tail for bit in range(bits_z)]


class Total:
    def __init__(self, place, copies, terms, landing):
        self.place, self.made, self.terms, self.landing = place, copies, terms, landing
        self.stages = len(place.partners())

    def copy(self, stage):
        device = self.place.partners()[stage]
        return self.made.far(("total", stage), self.terms.at[stage], self.landing.at[stage], device)

    def begin(self, stage):
        self.copy(stage).start()

    def finish(self, stage):
        self.copy(stage).wait()
        self.terms[stage + 1] = self.terms[stage] + self.landing[stage]


def one_hot(slots, count):
    rows = lax.broadcasted_iota(jnp.int32, (count, slots.shape[1]), 0)
    return jnp.where(rows == slots, 1.0, 0.0).astype(BF16)


def pick_rows(picked, slots, values):
    picked[...] = dot(one_hot(slots, picked.shape[0]), values).astype(BF16)


def find_slots(slots, ids_ref, core):
    n = ids_ref.shape[1]
    ids = ids_ref[...]
    second = jnp.where(ids == 1, 1.0, 0.0)
    earlier = lax.broadcasted_iota(jnp.int32, (n, n), 0) <= lax.broadcasted_iota(jnp.int32, (n, n), 1)
    before = dot(
        jnp.broadcast_to(second, (16, n)).astype(BF16), jnp.where(earlier, 1.0, 0.0).astype(BF16)
    )[0:1].astype(jnp.int32)
    rank = jnp.where(ids == 1, before - 1, lax.broadcasted_iota(jnp.int32, (1, n), 1) - before)
    own = ids == core
    slots[0:1, :] = jnp.where(own, rank, -1)
    slots[1:2, :] = jnp.where(own, -1, rank)
    slots[2:8, :] = jnp.full((6, n), -1, jnp.int32)
    return jnp.sum(second, axis=1, keepdims=True)


GAIN, SHIFT, ATTN_BIAS, OUT_BIAS, IN_BIAS, DIGITS = 0, 2, 4, 7, 9, 11


def pack_small(small, refs, count_second):
    small[...] = jnp.zeros_like(small)
    for row, ref in zip((GAIN, SHIFT, ATTN_BIAS, OUT_BIAS, IN_BIAS), refs):
        count, share = ref.shape
        small[row : row + count, :share] = ref[...].astype(F32)
    high = jnp.floor(count_second * (1 / 32))
    lane = lax.broadcasted_iota(jnp.int32, (1, 128), 1)
    small[DIGITS : DIGITS + 1, :] = jnp.where(lane == 0, high, jnp.where(lane == 1, count_second - 32 * high, 0.0))


def spread(shares, length, share, place_of):
    devices = shares.shape[0]
    lanes = lax.broadcasted_iota(jnp.int32, (128, length), 1)
    repeat = jnp.where(lax.rem(lanes, share) == lax.broadcasted_iota(jnp.int32, (128, length), 0), 1.0, 0.0)
    copies = dot(shares, repeat.astype(BF16))
    lanes = lax.broadcasted_iota(jnp.int32, (devices, length), 1)
    device = lax.broadcasted_iota(jnp.int32, (devices, length), 0)
    return jnp.sum(jnp.where(lax.div(lanes, share) == place_of(device), copies, 0.0), axis=0, keepdims=True)


def unpack_small(small_full, core, d, share, hidden_share, vectors, in_bias, out_bias, counts):
    nz, nx = small_full.shape[:2]
    devices = nz * nx * 2
    found = small_full[...].astype(F32).reshape(devices, 16, 128)

    def rows(row):
        return found[:, row, :].astype(BF16)

    def vector(shares):
        return spread(shares, d, share, lambda device: device)

    vectors[...] = jnp.zeros_like(vectors)
    for line, row, part in (
        (0, GAIN, 0), (0, GAIN + 1, 1), (0, ATTN_BIAS + 2, 2), (1, SHIFT, 0), (1, SHIFT + 1, 1),
        (2, ATTN_BIAS, 0), (2, ATTN_BIAS + 1, 2),
    ):
        vectors[line : line + 1, part * d : (part + 1) * d] = vector(rows(row))

    def of_expert(row):
        return jnp.where(core == 0, rows(row), rows(row + 1))

    out_bias[0:1, :] = vector(of_expert(OUT_BIAS))
    width = hidden_share * devices // CHUNKS
    tile = in_bias.shape[2]
    for chunk in range(CHUNKS):
        line = spread(
            of_expert(IN_BIAS), width, hidden_share,
            lambda device: jnp.where(lax.rem(device, 2) == chunk, lax.div(device, 2), -1),
        )
        for i in range(width // tile):
            in_bias[chunk * (width // tile) + i, 0:1, :] = line[:, i * tile : (i + 1) * tile]
    counts[...] = jnp.broadcast_to(jnp.sum(found[:, DIGITS, :], axis=0, keepdims=True), counts.shape)


def attend_pair(qkv, head, attended, log_total):
    n, d = attended.shape
    low = lax.broadcasted_iota(jnp.int32, (n, 128), 1) < HEAD
    one, zero = jnp.ones((), BF16), jnp.zeros((), BF16)
    query = qkv[:, pl.ds(pl.multiple_of(head * 128, 128), 128)]
    key = qkv[:, pl.ds(pl.multiple_of(d + head * 128, 128), 128)]
    value = qkv[:, pl.ds(pl.multiple_of(2 * d + head * 128, 128), 128)]
    values = [jnp.where(low, value, one), jnp.where(low, one, value)]
    queries = [jnp.where(low, query, zero), jnp.where(low, zero, query)]
    low = low[:BLOCK]
    allowed = lax.broadcasted_iota(jnp.int32, (BLOCK, BLOCK), 1) <= lax.broadcasted_iota(
        jnp.int32, (BLOCK, BLOCK), 0
    )
    for i in range(n // BLOCK):
        first, end = i * BLOCK, (i + 1) * BLOCK
        found = []
        for j in range(2):
            near = jnp.where(allowed, dot_last(queries[j][first:end], key[first:end]), MASKED)
            top = jnp.max(near, axis=-1, keepdims=True)
            if i:
                far = dot_last(queries[j][first:end], key[:first])
                top = jnp.maximum(top, jnp.max(far, axis=-1, keepdims=True))
            top = top * SCALE_LOG2
            out = dot(jnp.exp2(near * SCALE_LOG2 - top).astype(BF16), values[j][first:end])
            if i:
                out = out + dot(jnp.exp2(far * SCALE_LOG2 - top).astype(BF16), values[j][:first])
            found.append((out, top))
        (out_a, top_a), (out_b, top_b) = found
        total = pltpu.roll(jnp.where(low, out_b, out_a), HEAD, axis=1)
        attended[first:end, pl.ds(pl.multiple_of(head * 128, 128), 128)] = (
            jnp.where(low, out_a, out_b) / total
        ).astype(BF16)
        logs = (jnp.where(low, top_a, top_b) + jnp.log2(total)).T
        log_total[head, 0:1, first:end] = logs[0:1]
        log_total[head, 1:2, first:end] = logs[HEAD : HEAD + 1]


def gelu_and_slope(values):
    root = math.sqrt(2 / math.pi)
    cube = 0.044715
    square = values * values
    bent = jnp.tanh(values * (root + root * cube * square))
    half = 0.5 * (1 + bent)
    slope = half + 0.5 * values * (1 - bent * bent) * (root + 3 * root * cube * square)
    return values * half, slope


def norm_backward(values, gain, grad):
    scaled, inverse = row_stats(values)
    grad_scaled = grad * gain
    mean = jnp.mean(grad_scaled, axis=-1, keepdims=True)
    along = jnp.mean(grad_scaled * scaled, axis=-1, keepdims=True)
    term = inverse * (grad_scaled - mean - scaled * along)
    return term, jnp.sum(grad * scaled, axis=0, keepdims=True), jnp.sum(grad, axis=0, keepdims=True)


def attend_pair_backward(qkv, head, attended, grad, log_total, projected, turned):
    n, d = attended.shape
    low = lax.broadcasted_iota(jnp.int32, (n, 128), 1) < HEAD
    zero = jnp.zeros((), BF16)

    def columns(part):
        return pl.ds(pl.multiple_of(part * d + head * 128, 128), 128)

    query, key, value = (qkv[:, columns(part)] for part in range(3))
    grad = grad[:, columns(0)]
    product = (attended[:, columns(0)].astype(F32) * grad.astype(F32)).T
    inner = [jnp.sum(product[j * HEAD : (j + 1) * HEAD], axis=0, keepdims=True) for j in range(2)]
    logs = [log_total[head, j : j + 1, :] for j in range(2)]
    key_turned = key.T
    keys = [jnp.where(low, key, zero), jnp.where(low, zero, key)]
    values = [jnp.where(low, value, zero), jnp.where(low, zero, value)]
    low = low[:BLOCK]
    allowed = lax.broadcasted_iota(jnp.int32, (BLOCK, BLOCK), 0) <= lax.broadcasted_iota(
        jnp.int32, (BLOCK, BLOCK), 1
    )
    for i in range(n // BLOCK):
        first, end = i * BLOCK, (i + 1) * BLOCK
        found = []
        for j in range(2):
            grad_key = grad_value = 0.0
            for start, stop in ((first, end), (end, n)):
                if start == stop:
                    continue
                scores = dot_last(keys[j][first:end], query[start:stop])
                weights = jnp.exp2(scores * SCALE_LOG2 - logs[j][:, start:stop])
                if start == first:
                    weights = jnp.where(allowed, weights, 0.0)
                grad_weights = dot_last(values[j][first:end], grad[start:stop])
                grad_scores = (weights * (grad_weights - inner[j][:, start:stop])).astype(BF16)
                grad_value = grad_value + dot(weights.astype(BF16), grad[start:stop])
                grad_key = grad_key + dot(grad_scores, query[start:stop])
                part = dot(key_turned[j * HEAD : (j + 1) * HEAD, first:end], grad_scores)
                if i == 0:
                    turned[j * HEAD : (j + 1) * HEAD, start:stop] = part
                else:
                    turned[j * HEAD : (j + 1) * HEAD, start:stop] += part
            found.append((grad_key, grad_value))
        (key_a, value_a), (key_b, value_b) = found
        projected[first:end, columns(1)] = (jnp.where(low, key_a, key_b) * SCORE_SCALE).astype(BF16)
        projected[first:end, columns(2)] = jnp.where(low, value_a, value_b).astype(BF16)
    projected[:, columns(0)] = (turned[...].T * SCORE_SCALE).astype(BF16)


def block_kernel(nz, nx, tokens, cotangent, ids, small, w_qkv, w_out, in_own, hidden_own):
    n, d = tokens.shape
    heads = d // 128
    depth = w_qkv.shape[0]
    share = small[0].shape[1]
    hidden_share = hidden_own.shape[1]
    width = in_own.shape[3]
    tile = nx * hidden_share
    tiles = width // tile
    count = 2 * MOST
    cut = width // CUTS
    hidden_cut = hidden_share // CUTS
    in_tail, hidden_tail = (2, depth, cut), (hidden_cut, d)
    small_rows = 10 + EXPERTS * CHUNKS * (width // d)
    small_rows += -small_rows % 8

    def bf16(*shape):
        return jax.ShapeDtypeStruct(shape, BF16)

    def f32(*shape):
        return jax.ShapeDtypeStruct(shape, F32)

    outputs = dict(
        block_out=bf16(n, d),
        grad_res=f32(n, d),
        projected=bf16(n, 3 * d),
        qkv_terms=bf16(nz, nx, 2, depth, 3 * d),
        wo_terms=bf16(nz, nx, 2, depth, d),
        in_sum=bf16(CHUNKS, EXPERTS, depth, width),
        hidden_sum=bf16(EXPERTS, hidden_share, d),
        qkv_full=bf16(nz, nx, 2, depth, 3 * d),
        wo_full=bf16(nz, nx, 2, depth, d),
        grad_rows=bf16(2, MOST, d),
        rows=bf16(2, MOST, d),
        made_rows=bf16(2, MOST, d),
        back_rows=bf16(2, MOST, d),
        in_full=bf16(CHUNKS, nz, nx, 2, depth, width),
        hidden_full=bf16(CHUNKS, nz, nx, hidden_share, d),
        in_terms=bf16(CHUNKS, nz, nx, 2, depth, width),
        hidden_terms=bf16(CHUNKS, nz, nx, hidden_share, d),
        normed=bf16(n, d),
        qkv=bf16(n, 3 * d),
        attended=bf16(n, d),
        logs=f32(heads, 8, n),
        residual=f32(n, d),
    )
    small_outputs = dict(small_terms=f32(small_rows, d), vectors=f32(8, 3 * d), counts=f32(8, 128))

    landings = []
    for _ in range(CHUNKS):
        landings += [landing_shapes(nz, nx, in_tail, False)] * CUTS
        landings += [landing_shapes(nz, nx, hidden_tail, False)] * CUTS
    per_piece = len(landings[0])
    landing_scratch = [pltpu.VMEM(shape, BF16) for shapes in landings for shape in shapes]
    spares = [pltpu.VMEM((2,) + landings[0][0], BF16), pltpu.VMEM((2,) + landings[CUTS][0], BF16)]

    names = list(outputs) + list(small_outputs)

    def kernel(*refs):
        (
            tokens_hbm, cot_hbm, ids_ref, gain_ref, shift_ref, attn_bias_ref, out_bias_ref, in_bias_ref,
            qkv_own, wo_own, in_own, hidden_own,
        ) = refs[:12]
        out = dict(zip(names, refs[12 : 12 + len(names)]))
        rest = refs[12 + len(names) :]
        slots, small_own, small_full, in_bias, out_bias, bias_sums = rest[:6]
        spare_in, spare_hidden = rest[6:8]
        landing = rest[8 : 8 + len(landing_scratch)]
        made = Copies(*rest[8 + len(landing_scratch) :])

        place = Place(nz, nx)
        z, xy, core = place.z, place.xy, place.core
        vectors, sums = out["vectors"], out["small_terms"]

        def columns_of(ref, part):
            return lambda zs, xs: [ref.at[zs, xs, core, :, pl.ds(part * d, d)]]

        def with_small(zs, xs):
            return [out["qkv_full"].at[zs, xs, core, :, pl.ds(2 * d, d)], small_full.at[zs, xs, core]]

        regions = [columns_of(out["qkv_full"], 0), columns_of(out["qkv_full"], 1), with_small, columns_of(out["wo_full"], 0)]
        gathered = [(region, region(ALL, ALL)) for region in regions]
        for chunk in range(CHUNKS):
            for i in range(CUTS):
                gathered.append(
                    (lambda zs, xs, chunk=chunk, i=i: [out["in_full"].at[chunk, zs, xs, :, :, pl.ds(i * cut, cut)]], None)
                )
            for i in range(CUTS):
                gathered.append(
                    (
                        lambda zs, xs, chunk=chunk, i=i: [
                            out["hidden_full"].at[chunk, zs, xs, pl.ds(i * hidden_cut, hidden_cut)]
                        ],
                        None,
                    )
                )
        gather = Gather("gather", place, made, gathered)

        pieces = []
        for chunk in range(CHUNKS):
            for i in range(2 * CUTS):
                at = len(pieces)
                mine = landing[at * per_piece : (at + 1) * per_piece]
                if i < CUTS:
                    at_columns = pl.ds(i * cut, cut)
                    pieces.append(
                        (
                            lambda zs, xs, _, c=chunk, s=at_columns: out["in_terms"].at[c, zs, xs, :, :, s],
                            mine,
                            spare_in.at[at % 2],
                            lambda expert, c=chunk, s=at_columns: out["in_sum"].at[c, expert, :, s],
                            "both",
                        )
                    )
                else:
                    at_rows = pl.ds((i - CUTS) * hidden_cut, hidden_cut)
                    pieces.append(
                        (
                            lambda zs, xs, _, c=chunk, s=at_rows: out["hidden_terms"].at[c, zs, xs, s],
                            mine,
                            spare_hidden.at[at % 2],
                            lambda expert, s=at_rows: out["hidden_sum"].at[expert, s],
                            chunk,
                        )
                    )
        reduce = Reduce("reduce", place, made, pieces)

        near = [
            made.local("own qkv", qkv_own, out["qkv_full"].at[z, xy, core]),
            made.local("own wo", wo_own, out["wo_full"].at[z, xy, core]),
        ]
        late = [made.local("own hidden", hidden_own.at[core], out["hidden_full"].at[core, z, xy])]
        pair = [
            made.far("pair hidden", hidden_own.at[1 - core], out["hidden_full"].at[core, z, xy], place.sibling())
        ]
        for chunk in range(CHUNKS):
            late.append(made.local(("own in", chunk), in_own.at[chunk, core], out["in_full"].at[chunk, z, xy, core]))
            pair.append(
                made.far(
                    ("pair in", chunk), in_own.at[chunk, 1 - core], out["in_full"].at[chunk, z, xy, core], place.sibling()
                )
            )
        for copy in near + late:
            copy.start()
        place.barrier()
        for copy in near:
            copy.wait()

        def first_phase(cot, picked):
            load = made.local("cot", cot_hbm, cot)
            load.start()
            gather.tick(0)
            for copy in pair:
                copy.start()
            count_second = find_slots(slots, ids_ref, core)
            pack_small(small_own, (gain_ref, shift_ref, attn_bias_ref, out_bias_ref, in_bias_ref), count_second)
            small_full[z, xy, core] = small_own[...].astype(BF16)
            gather.tick(1)
            load.wait()
            pick_rows(picked.at[1], slots[1:2, :], cot[...])
            theirs = made.far("grad rows", picked.at[1], out["grad_rows"].at[1], place.sibling())
            theirs.start()
            gather.tick(2)
            pick_rows(picked.at[0], slots[0:1, :], cot[...])
            mine = made.local("grad rows", picked.at[0], out["grad_rows"].at[0])
            mine.start()
            for copy in late + pair:
                copy.wait()
            gather.tick(3)
            mine.wait()
            theirs.wait()

        pl.run_scoped(first_phase, pltpu.VMEM((n, d), BF16), pltpu.VMEM((2, MOST, d), BF16))

        def forward_phase(tok, w, wo, normed, qkv, attended, logs, residual, normed_two, picked):
            load = made.local("tokens", tokens_hbm, tok)
            load.start()
            loads = []
            for part in range(3):
                gather.tick(4 + part)
                gather.need(part)
                at_columns = pl.ds(part * d, d)
                loads.append(
                    made.local(
                        ("w", part), out["qkv_full"].at[:, :, :, :, at_columns], w.at[:, :, :, :, at_columns]
                    )
                )
                loads[-1].start()
            unpack_small(small_full, core, d, share, hidden_share, vectors, in_bias, out_bias, out["counts"])
            load.wait()
            for copy in loads:
                copy.wait()

            @pl.loop(0, n // BLOCK)
            def _(i):
                rows = pl.ds(pl.multiple_of(i * BLOCK, BLOCK), BLOCK)
                scaled, _ = row_stats(tok[rows].astype(F32))
                normed[rows] = (scaled * vectors[0:1, :d] + vectors[1:2, :d]).astype(BF16)
                weight = as_rows(w[...], d)
                qkv[rows] = (dot(normed[rows], weight) + vectors[2:3, :]).astype(BF16)
                ticks_at(i, {1: 7, 3: 8}, gather)

            saves = [
                made.local("save normed", normed, out["normed"]),
                made.local("save qkv", qkv, out["qkv"]),
            ]
            for save in saves:
                save.start()

            @pl.loop(0, heads)
            def _(head):
                attend_pair(qkv, head, attended, logs)
                ticks_at(head, {2: 9, 4: 10, 6: 11}, gather)

            saves += [
                made.local("save attended", attended, out["attended"]),
                made.local("save logs", logs, out["logs"]),
            ]
            for save in saves[2:]:
                save.start()
            gather.need(3)
            load_wo = made.local("wo", out["wo_full"], wo)
            load_wo.start()
            gather.tick(12)
            load_wo.wait()

            @pl.loop(0, n // BLOCK)
            def _(i):
                rows = pl.ds(pl.multiple_of(i * BLOCK, BLOCK), BLOCK)
                added = dot(attended[rows], as_rows(wo[...], d)) + vectors[0:1, 2 * d :]
                residual[rows] = tok[rows].astype(F32) + added
                scaled, _ = row_stats(residual[rows])
                normed_two[rows] = (scaled * vectors[0:1, d : 2 * d] + vectors[1:2, d : 2 * d]).astype(BF16)
                ticks_at(i, {1: 13}, gather)

            saves.append(made.local("save residual", residual, out["residual"]))
            saves[-1].start()
            pick_rows(picked.at[1], slots[1:2, :], normed_two[...])
            theirs = made.far("rows", picked.at[1], out["rows"].at[1], place.sibling())
            theirs.start()
            pick_rows(picked.at[0], slots[0:1, :], normed_two[...])
            saves.append(made.local("rows", picked.at[0], out["rows"].at[0]))
            saves[-1].start()
            gather.tick(14)
            for save in saves:
                save.wait()
            theirs.wait()

        pl.run_scoped(
            forward_phase,
            pltpu.VMEM((n, d), BF16),
            pltpu.VMEM((nz, nx, 2, depth, 3 * d), BF16),
            pltpu.VMEM((nz, nx, 2, depth, d), BF16),
            pltpu.VMEM((n, d), BF16),
            pltpu.VMEM((n, 3 * d), BF16),
            pltpu.VMEM((n, d), BF16),
            pltpu.VMEM((heads, 8, n), F32),
            pltpu.VMEM((n, d), F32),
            pltpu.VMEM((n, d), BF16),
            pltpu.VMEM((2, MOST, d), BF16),
        )

        def expert_phase(rows, grads, turned, made_total, back_total, w_in, w_hidden, grad_in, grad_hidden):
            loads = [
                made.local("load rows", out["rows"], rows),
                made.local("load grads", out["grad_rows"], grads),
            ]
            for copy in loads:
                copy.start()

            def weights(step):
                slot, chunk, t = lax.rem(step, 2), lax.div(step, tiles), lax.rem(step, tiles)
                at_columns = pl.ds(pl.multiple_of(t * tile, tile), tile)
                return [
                    made.local("w in", out["in_full"].at[chunk, :, :, :, :, at_columns], w_in.at[slot]),
                    made.local("w hidden", out["hidden_full"].at[chunk, t], w_hidden.at[slot]),
                ]

            def stores(step):
                slot, chunk, t = lax.rem(step, 2), lax.div(step, tiles), lax.rem(step, tiles)
                at_columns = pl.ds(pl.multiple_of(t * tile, tile), tile)
                return [
                    made.local("store in", grad_in.at[slot], out["in_terms"].at[chunk, :, :, :, :, at_columns], slot),
                    made.local("store hidden", grad_hidden.at[slot], out["hidden_terms"].at[chunk, t], slot),
                ]

            made_total[...] = jnp.zeros_like(made_total)
            back_total[...] = jnp.zeros_like(back_total)
            for copy in loads:
                copy.wait()
            turned[...] = as_rows(rows[...], count).T
            total = jnp.sum(as_rows(grads[...], count).astype(F32), axis=0, keepdims=True)
            sums[...] = jnp.zeros_like(sums)
            for expert in range(EXPERTS):
                sums[8 + expert : 9 + expert, :] = jnp.where(core == expert, total, 0.0)

            @pl.loop(0, CHUNKS * tiles)
            def _(step):
                slot = lax.rem(step, 2)
                for chunk in range(CHUNKS):
                    @pl.when(step == chunk * tiles)
                    def _(chunk=chunk):
                        for piece in range(2 * CUTS):
                            gather.need(4 + chunk * 2 * CUTS + piece)
                        for copy in weights(step):
                            copy.start()
                        if chunk:
                            reduce.tick(0)

                for copy in weights(step):
                    copy.wait()

                @pl.when(lax.rem(step, tiles) != tiles - 1)
                def _():
                    for copy in weights(step + 1):
                        copy.start()

                def beside(spot):
                    ticks_at(step, {k: now for (k, at), now in gather_beside.items() if at == spot}, gather)
                    ticks_at(step, {k: now for (k, at), now in reduce_beside.items() if at == spot}, reduce)

                rows_now, grads_now = as_rows(rows[...], count), as_rows(grads[...], count)
                w_in_now = as_rows(w_in[slot], d)
                w_hidden_now = as_rows(w_hidden[slot], tile)
                hidden_pre = dot(rows_now, w_in_now) + in_bias[step, 0:1, :]
                hidden, slope = gelu_and_slope(hidden_pre)
                hidden = hidden.astype(BF16)
                grad_pre = dot_last(grads_now, w_hidden_now) * slope
                bias_sums[step, 0:1, :] = jnp.sum(grad_pre, axis=0, keepdims=True)
                grad_pre = grad_pre.astype(BF16)
                beside(0)
                made_total[...] += dot(hidden, w_hidden_now)
                back_total[...] += dot_last(grad_pre, w_in_now)
                beside(1)

                @pl.when(lax.rem(step, tiles) >= 2)
                def _():
                    for copy in stores(step - 2):
                        copy.wait()

                grad_hidden[slot] = split_rows(dot(hidden.T, grads_now).astype(BF16), (nx, hidden_share, d))
                grad_in[slot] = split_rows(dot(turned[...], grad_pre).astype(BF16), (nz, nx, 2, depth, tile))
                for copy in stores(step):
                    copy.start()
                beside(2)

                @pl.when(lax.rem(step, tiles) == tiles - 1)
                def _():
                    if tiles > 1:
                        for copy in stores(step - 1):
                            copy.wait()
                    for copy in stores(step):
                        copy.wait()

            rows[...] = split_rows((made_total[...] + out_bias[0:1, :]).astype(BF16), (2, MOST, d))
            grads[...] = split_rows(back_total[...].astype(BF16), (2, MOST, d))
            results = []
            for name, source in (("made_rows", rows), ("back_rows", grads)):
                results.append(made.far(name, source.at[1], out[name].at[1], place.sibling()))
                results.append(made.local(name, source.at[0], out[name].at[0]))
            for copy in results:
                copy.start()
            reduce.tick(reduce_next[0])
            for copy in results:
                copy.wait()

        gather_beside = {(k // 2, k % 2 * 2): 15 + k for k in range(8)}
        reduce_beside = {(tiles, 2): 1, (tiles + 1, 2): 2, (tiles + 2, 2): 3, (tiles + 3, 2): 4}
        reduce_next = [5]
        pl.run_scoped(
            expert_phase,
            pltpu.VMEM((2, MOST, d), BF16),
            pltpu.VMEM((2, MOST, d), BF16),
            pltpu.VMEM((d, count), BF16),
            pltpu.VMEM((count, d), F32),
            pltpu.VMEM((count, d), F32),
            pltpu.VMEM((2, nz, nx, 2, depth, tile), BF16),
            pltpu.VMEM((2, nx, hidden_share, d), BF16),
            pltpu.VMEM((2, nz, nx, 2, depth, tile), BF16),
            pltpu.VMEM((2, nx, hidden_share, d), BF16),
        )
        reduce_next[0] += 1

        def backward_phase(
            grad_res, made_rows, back_rows, cot, wo, att, qkv, logs, normed, block, branch, grad_att, turned, projected, wide,
            slots_turned,
        ):
            def load(name, source, target):
                copy = made.local(("back", name), source, target)
                copy.start()
                return copy

            loads = [
                load("residual", out["residual"], grad_res),
                load("made", out["made_rows"], made_rows),
                load("back", out["back_rows"], back_rows),
                load("cot", cot_hbm, cot),
                load("wo", out["wo_full"], wo),
            ]
            late_loads = [
                load("att", out["attended"], att),
                load("qkv", out["qkv"], qkv),
                load("logs", out["logs"], logs),
                load("normed", out["normed"], normed),
            ]
            slots_turned[...] = slots[...].astype(F32).T
            for copy in loads:
                copy.wait()

            @pl.loop(0, n // BLOCK)
            def _(i):
                rows = pl.ds(pl.multiple_of(i * BLOCK, BLOCK), BLOCK)
                columns = lax.broadcasted_iota(jnp.int32, (BLOCK, MOST), 1).astype(F32)
                chosen = jnp.concatenate(
                    [jnp.where(columns == slots_turned[rows, k : k + 1], 1.0, 0.0).astype(BF16) for k in range(2)],
                    axis=1,
                )
                values = grad_res[rows]
                block[rows] = (values + dot(chosen, as_rows(made_rows[...], count))).astype(BF16)
                grad = dot(chosen, as_rows(back_rows[...], count))
                term, gain_sum, shift_sum = norm_backward(values, vectors[0:1, d : 2 * d], grad)
                sums[1:2, :] += gain_sum
                sums[3:4, :] += shift_sum
                total = cot[rows].astype(F32) + term
                grad_res[rows] = total
                low = total.astype(BF16)
                branch[rows] = low
                sums[6:7, :] += jnp.sum(low.astype(F32), axis=0, keepdims=True)
                grad_att[rows] = dot_last(low, as_rows(wo[...], d)).astype(BF16)
                ticks_at(i, {1: reduce_next[0], 3: reduce_next[0] + 1}, reduce)

            now = reduce_next[0] + 2
            saves = [load("block", block, out["block_out"]), load("grad_res", grad_res, out["grad_res"])]
            for copy in late_loads:
                copy.wait()

            @pl.loop(0, heads)
            def _(head):
                attend_pair_backward(qkv, head, att, grad_att, logs, projected, turned)
                spots = [heads // 8, heads // 4, heads // 2, heads * 5 // 8, heads - 1]
                ticks_at(head, {spot: now + k for k, spot in enumerate(spots)}, reduce)

            now += 5
            saves.append(load("projected", projected, out["projected"]))
            wide[0] = split_rows(dot(att[...].T, branch[...]).astype(BF16), wide.shape[1:])
            written = [load("wo terms", wide.at[0], out["wo_terms"])]
            normed_turned = normed[...].T
            for part in range(3):
                columns = slice(part * d, (part + 1) * d)
                spot = (part + 1) % 2
                if part > 0:
                    written[part - 1].wait()
                wide[spot] = split_rows(dot(normed_turned, projected[:, columns]).astype(BF16), wide.shape[1:])
                written.append(
                    load(("qkv terms", part), wide.at[spot], out["qkv_terms"].at[:, :, :, :, pl.ds(part * d, d)])
                )
                if part != 1:
                    sums[4 + part // 2 : 5 + part // 2, :] = jnp.sum(
                        projected[:, columns].astype(F32), axis=0, keepdims=True
                    )
                reduce.tick(now)
                now += 1
            lines = width // d
            for step in range(CHUNKS * tiles):
                first = (step % tiles) * tile
                for expert in range(EXPERTS):
                    row = 10 + expert * CHUNKS * lines + step // tiles * lines + first // d
                    sums[row : row + 1, first % d : first % d + tile] = jnp.where(
                        core == expert, bias_sums[step, 0:1, :], 0.0
                    )
            while now < len(pieces) + reduce.stages(pieces[0]) - 1:
                reduce.tick(now)
                now += 1
            for piece in range(len(pieces)):
                reduce.need(piece)
            for copy in saves + written[2:]:
                copy.wait()

        pl.run_scoped(
            backward_phase,
            pltpu.VMEM((n, d), F32),
            pltpu.VMEM((2, MOST, d), BF16),
            pltpu.VMEM((2, MOST, d), BF16),
            pltpu.VMEM((n, d), BF16),
            pltpu.VMEM((nz, nx, 2, depth, d), BF16),
            pltpu.VMEM((n, d), BF16),
            pltpu.VMEM((n, 3 * d), BF16),
            pltpu.VMEM((heads, 8, n), F32),
            pltpu.VMEM((n, d), BF16),
            pltpu.VMEM((n, d), BF16),
            pltpu.VMEM((n, d), BF16),
            pltpu.VMEM((n, d), BF16),
            pltpu.VMEM((128, n), F32),
            pltpu.VMEM((n, 3 * d), BF16),
            pltpu.VMEM((2, nz, nx, 2, depth, d), BF16),
            pltpu.VMEM((n, 8), F32),
        )

    exchanged = nz + nx
    results = pl.pallas_call(
        kernel,
        out_shape=list(outputs.values()) + list(small_outputs.values()),
        in_specs=[HBM, HBM] + [VMEM] * 6 + [HBM] * 4,
        out_specs=[HBM] * len(outputs) + [VMEM] * len(small_outputs),
        scratch_shapes=[
            pltpu.VMEM((8, n), jnp.int32),
            pltpu.VMEM((16, 128), F32),
            pltpu.VMEM((nz, nx, 2, 16, 128), BF16),
            pltpu.VMEM((CHUNKS * tiles, 8, tile), F32),
            pltpu.VMEM((8, d), F32),
            pltpu.VMEM((CHUNKS * tiles, 8, tile), F32),
            *spares,
            *landing_scratch,
            *semaphores(36 * exchanged + 32, 16 * (nx // 2 + 2) + 48),
        ],
        compiler_params=pltpu.CompilerParams(
            collective_id=1, has_side_effects=True, vmem_limit_bytes=64 * MIB - 64 * 1024
        ),
        name="block",
    )(tokens, cotangent, ids, *small, w_qkv, w_out, in_own, hidden_own)
    return dict(zip(names, results))


def ticks_at(step, wanted, stream):
    for k, now in wanted.items():
        @pl.when(step == k)
        def _(now=now):
            stream.tick(now)


def last_kernel(nz, nx, block, tokens):
    n, d = tokens.shape
    depth = block["wo_terms"].shape[3]
    tail = (depth, d)
    landings = [landing_shapes(nz, nx, tail, True)] * 4
    per_piece = len(landings[0])
    landing_scratch = [pltpu.VMEM(shape, BF16) for shapes in landings for shape in shapes]
    partners = nz.bit_length() - 1 + nx.bit_length() - 1 + 1
    shape = block["small_terms"].shape

    def kernel(
        projected_ref, w_ref, grad_ref, tokens_ref, vectors, small_ref, qkv_terms, wo_terms,
        input_grad, small_sum, qkv_sum, wo_sum, terms, terms_landing, spare, *scratch,
    ):
        place = Place(nz, nx)
        made = Copies(*scratch[-3:])

        def piece(at, i):
            mine = scratch[at * per_piece : (at + 1) * per_piece]
            if i == 3:
                return lambda zs, xs, core: wo_terms.at[zs, xs, core], mine, spare.at[at % 2], wo_sum, "first"
            columns = pl.ds(i * d, d)
            return (
                lambda zs, xs, core: qkv_terms.at[zs, xs, core, :, columns],
                mine, spare.at[at % 2], qkv_sum.at[:, columns], "first",
            )

        reduce = Reduce("last", place, made, [piece(at, i) for at, i in enumerate((3, 0, 1, 2))])
        total = Total(place, made, terms, terms_landing)
        place.barrier()
        reduce.tick(0)
        terms[0] = small_ref[...]

        @pl.loop(0, n // BLOCK)
        def _(i):
            rows = pl.ds(pl.multiple_of(i * BLOCK, BLOCK), BLOCK)
            grad = dot_last(projected_ref[rows], as_rows(w_ref[...], d))
            term, gain_sum, shift_sum = norm_backward(tokens_ref[rows].astype(F32), vectors[0:1, :d], grad)
            input_grad[rows] = grad_ref[rows] + term
            terms[0, 0:1, :] += gain_sum
            terms[0, 2:3, :] += shift_sum
            ticks_at(i, {1: 1, 3: 2}, reduce)

        stage = 0
        for now in range(3, 3 + reduce.stages(reduce.pieces[0])):
            if stage < total.stages:
                total.begin(stage)
            reduce.tick(now)
            if stage < total.stages:
                total.finish(stage)
                stage += 1
        for late in range(stage, total.stages):
            total.begin(late)
            total.finish(late)
        for at in range(4):
            reduce.need(at)
        small_sum[...] = terms[total.stages]

    return pl.pallas_call(
        kernel,
        out_shape=[
            jax.ShapeDtypeStruct((n, d), F32),
            jax.ShapeDtypeStruct(shape, F32),
            jax.ShapeDtypeStruct((depth, 3 * d), BF16),
            jax.ShapeDtypeStruct((depth, d), BF16),
        ],
        in_specs=[VMEM] * 6 + [HBM] * 2,
        out_specs=[VMEM] * 2 + [HBM] * 2,
        scratch_shapes=[
            pltpu.VMEM((partners + 1,) + shape, F32),
            pltpu.VMEM((partners,) + shape, F32),
            pltpu.VMEM((2,) + landings[0][0], BF16),
            *landing_scratch,
            *semaphores(4 * (2 * nx + nz) + partners, 4 * (nx + 1)),
        ],
        compiler_params=pltpu.CompilerParams(collective_id=2, has_side_effects=True, vmem_limit_bytes=60 * MIB),
        name="last_sums",
    )(
        block["projected"], block["qkv_full"], block["grad_res"], tokens, block["vectors"], block["small_terms"],
        block["qkv_terms"], block["wo_terms"],
    )


def shards(
    nz, nx, tokens, norm_gain, norm_bias, w_qkv, attn_bias, w_attn_out, expert_in, expert_in_bias, expert_out,
    expert_out_bias, expert_ids, running_load, cotangent,
):
    n, d = tokens.shape
    devices = nz * nx * 2
    chips = nz * nx
    core = lax.axis_index("core")
    me = lax.axis_index(("dp", "xy", "core"))
    share = norm_gain.shape[1]
    depth, width = expert_in.shape[1:]
    hidden_share = expert_out.shape[1]

    def columns(chip, chunk):
        first = (chip * CHUNKS + chunk) * hidden_share
        return expert_in[:, :, first : first + hidden_share]

    in_own = jnp.stack(
        [jnp.concatenate([columns(chip, chunk) for chip in range(chips)], axis=2) for chunk in range(CHUNKS)]
    )
    small = (norm_gain, norm_bias, attn_bias, expert_out_bias, expert_in_bias)
    block = block_kernel(
        nz, nx, tokens, cotangent, expert_ids.reshape(1, n), small, w_qkv, w_attn_out, in_own, expert_out
    )
    input_grad, small_sum, qkv_sum, wo_sum = last_kernel(nz, nx, block, tokens)

    mine = lax.dynamic_slice_in_dim(small_sum[:10], me * share, share, axis=1)
    lines = width // CHUNKS // d
    in_bias_sum = small_sum[10 : 10 + EXPERTS * CHUNKS * lines].reshape(EXPERTS, CHUNKS, width // CHUNKS)
    in_bias_sum = lax.dynamic_slice(
        in_bias_sum, (0, core, me // CHUNKS * hidden_share), (EXPERTS, 1, hidden_share)
    )[:, 0]
    in_sum = block["in_sum"].reshape(CHUNKS, EXPERTS, depth, chips, hidden_share)
    in_sum = in_sum.transpose(1, 2, 3, 0, 4).reshape(EXPERTS, depth, width).astype(F32)
    counts = block["counts"][0, :2]
    total_second = (counts[0] * 32 + counts[1]).astype(jnp.int32)
    expert_counts = jnp.stack([n * devices - total_second, total_second])
    expert_load = 0.9 * running_load + 0.1 * (expert_counts.astype(F32) * EXPERTS / (n * devices))
    return (
        block["block_out"],
        input_grad,
        mine[0:2],
        mine[2:4],
        qkv_sum.astype(F32),
        mine[4:7],
        wo_sum.astype(F32),
        in_sum,
        in_bias_sum,
        block["hidden_sum"].astype(F32),
        mine[8:10],
        expert_counts,
        expert_load,
    )


def solution(mesh):
    nz, nx = mesh.shape["dp"], mesh.shape["fsdp"] // 2
    fine = Mesh(mesh.devices.reshape(nz, nx, 2), ("dp", "xy", "core"))
    every = ("dp", "xy", "core")
    row, column, middle = P(every, None), P(None, every), P(None, every, None)
    return jax.shard_map(
        functools.partial(shards, nz, nx),
        mesh=fine,
        in_specs=(
            row, column, column, row, column, row, middle, column, middle, column, row, P(), row,
        ),
        out_specs=(row, row, column, column, row, column, row, middle, column, middle, column, P(), P()),
        check_vma=False,
    )
```

time: 2250 us -> 491 us (0.22)
  waiting for transfers between devices: 1180 us -> 0 us
  Pallas kernels: 0 us -> 453 us
  matrix products: 421 us -> 0 us
  blocking collectives: 272 us -> 0 us
  other arithmetic: 213 us -> 7.56 us
  local copies, waits for them, and re-layouts: 118 us -> 24.5 us
    reduce_scatter x6 -> x0, waiting for transfers between devices: 1040 us -> none  [the longest x2 371 us: shards(): lax.psum_scatter(grad_terms[0], ('dp', 'fsdp'), scatter_dimension=0, tile...]
    pallas_call x0 -> x2, Pallas kernels: none -> 453 us  [the longest x1 381 us: block_kernel(): pl.pallas_call(kernel, out_shape=list(outputs.values()) + list(small_outp...]
    dot_general x32 -> x0, matrix products: 421 us -> none  [the longest x6 75.8 us: contract_rows(): lax.dot_general(left_side, right_side, (((0,), (0,)), ((), ())), preferre...]
    all_gather x5 -> x0, blocking collectives: 193 us -> none  [the longest x2 79.8 us: shards(): lax.all_gather(expert_in_bias[expert], ('dp', 'fsdp'), axis=0, tiled=True)]
    unnamed x18 -> x0, waiting for transfers between devices: 143 us -> none
    unnamed x2 -> x0, blocking collectives: 79.1 us -> none
    reduce_sum x17 -> x0, other arithmetic: 67.6 us -> none  [the longest x2 30.7 us: one_block(): row_total = jnp.sum(weights, axis=-1, keepdims=True)]
    convert_element_type x13 -> x3, other arithmetic: 66.5 us -> 5.48 us  [the longest x1 2.27 us: shards(): block['hidden_sum'].astype(F32)]
  transfers between devices with their start and end apart: 15 -> 0, of which waited for: 8 -> 0; matrix products, arithmetic and copies ran while one was open for 19% -> 0% of each run, Pallas kernels for 0% -> 0%
where the time goes in v2:
time: 491 us; the launch traced here: 487 us
  Pallas kernels  453 us (92%)
  local copies, waits for them, and re-layouts  24.5 us (5%)
  other arithmetic  7.56 us (2%)
    pallas_call x1, Pallas kernels, block_kernel(): pl.pallas_call(kernel, out_shape=list(outputs.values()) + list(small_outp...  381 us
    pallas_call x1, Pallas kernels, last_kernel(): pl.pallas_call(kernel, out_shape=[jax.ShapeDtypeStruct((n, d), F32), jax....  71.7 us
    unnamed x25, local copies, waits for them, and re-layouts  15.4 us

profile of v2, /device:TPU:0, one launch (start us, length us, event | category | flops | bytes accessed | tf_op | source)
XLA Modules:
  0.0 487.1 jit_solution(2393039388723707993)
XLA Ops:
  3.6 0.8 constant_dynamic-update-slice_fusion.11
  4.4 0.8 constant_dynamic-update-slice_fusion.10
  5.1 0.8 constant_dynamic-update-slice_fusion.9
  5.9 0.8 constant_dynamic-update-slice_fusion.8
  6.6 0.8 constant_dynamic-update-slice_fusion.7
  7.4 0.8 constant_dynamic-update-slice_fusion.6
  8.1 0.8 constant_dynamic-update-slice_fusion.5
  8.9 0.8 constant_dynamic-update-slice_fusion.4
  10.4 0.8 constant_dynamic-update-slice_fusion.2
  11.9 0.8 constant_dynamic-update-slice_fusion
  14.1 0.8 pad_maximum_fusion.refs_10_
  14.9 381.1 %block.1 = (bf16[1024,1024]{1,0:T(8,128)(2,1)}, f32[1024,1024]{1,0:T(8,128)}, bf16[1024,3072]{1,0:T(8,128)(2,1)}, bf16[4,4,2,32,3072]{4,3,2,1,0:T(8,128)(2,1)}, ...) custom-call(bf16[1024,1024]{1,0:T(8,128)(2,1)} %tokens_ref.1, ...), custom_call_target="tpu_custom_call" | custom-call | tf_op jit(solution)/shard_map/block/pallas_call | solution.py:992
  396.0 1.3 fusion.1
  398.7 1.2 multiply_add_fusion
  399.9 71.7 %last_sums.1 = (f32[1024,1024]{1,0:T(8,128)}, f32[24,1024]{1,0:T(8,128)}, bf16[32,3072]{1,0:T(8,128)(2,1)}, bf16[32,1024]{1,0:T(8,128)(2,1)}) custom-call(bf16[1024,3072]{1,0:T(8,128)(2,1)} %get-tuple-element.29.projected_ref, bf16[4,4,2,32,3072]{4,3,2,1,0:T(8,128)(2,1)} %get-tuple-element.30.w_ref, f32[1024,1024]{1,0:T(8,128)} %get-tuple-element.31.grad_ref, ...), custom_call_target="tpu_custom_call" | custom-call | tf_op jit(solution)/shard_map/last_sums/pallas_call | solution.py:1081
  471.6 0.8 slice.161
  473.2 1.7 convert_element_type.28
  474.9 1.5 convert_element_type.29
  476.4 0.8 slice.157
  478.6 0.8 copy.26
  479.5 1.8 reshape.52
  481.3 2.3 convert_element_type.34
  483.5 1.3 copy.60
  484.9 2.0 copy.61
  (19 shorter events, 8.0 us)
Async XLA Ops:
  399.9 78.6 %copy-start.2 = (bf16[2,2,32,2048]{3,2,1,0:T(8,128)(2,1)S(1)}, bf16[2,2,32,2048]{3,2,1,0:T(8,128)(2,1)}, u32[]{:S(2)}) copy-start(bf16[2,2,32,2048]{3,2,1,0:T(8,128)(2,1)} %get-tuple-element.40) | copy-start | bytes 1572868
  472.5 11.0 %copy-start.1 = (bf16[1024,1024]{1,0:T(8,128)(2,1)S(1)}, bf16[1024,1024]{1,0:T(8,128)(2,1)}, u32[]{:S(2)}) copy-start(bf16[1024,1024]{1,0:T(8,128)(2,1)} %get-tuple-element.91) | copy-start | bytes 6291460
  481.3 3.6 copy-start
